TPU v7x, 512 devices: a whole 4x8x8 slice. The times are simulated.
512 devices in a mesh: date: 256 (over z, y, x), row: 2 (over core).
Axes of the slice: x: 4, y: 8, z: 8, core: 2. Of those that a mesh axis runs over, the one named last changes fastest.
Arguments:
- slc: bfloat16 [2, 256, 32, 1024], P(None, 'date', 'row'), may hold values from -6 to 6
- valid_rows: int32 [256, 32], P('date', 'row'), may hold values 0 or 1
- pair_order: int32 [256, 10], P('date'), may hold values from 0 to 9, each once within a row
Outputs:
- phase: bfloat16 [2, 256, 10, 32, 1024], P(None, 'date', None, 'row')
- coherence: bfloat16 [256, 10, 32, 1024], P('date', None, 'row')
Inputs may be any that keep to these rules, and one draw needn't show every extreme that they name: `pair_order`: each date's row holds every value from 0 to 9 once.
All inputs are finite; a program needn't handle non-finite values. No bound on the sum of `valid_rows` on one device may be relied on, other than what follows from the above.
Results may differ from a plain program's by a relative error of at most 0.001.
Values may be sent and summed in bfloat16 or wider, within the bound.
No kernel may reach another device: no remote copies, remote signals or barrier semaphores. Data moves between devices by JAX's collectives and lax.ppermute only.
A program may use at most 64 MiB of HBM per device.

v0:
```python
import jax
import jax.numpy as jnp
from jax import lax
from jax.sharding import PartitionSpec as P


def passed_along(shard, axis, by):
    length = lax.axis_size(axis)
    pairs = [(i, i + by) for i in range(length) if 0 <= i + by < length]
    return lax.ppermute(shard, axis, pairs)


def with_halo(cells, sides, width):
    for axis, dim in sides:
        count = lax.axis_size(axis)
        ends = count - 1
        head = lax.slice_in_dim(cells, 0, width, axis=dim)
        tail = lax.slice_in_dim(cells, cells.shape[dim] - width, cells.shape[dim], axis=dim)
        cells = jnp.concatenate(
            [
                lax.ppermute(tail, axis, [(i, (i + 1) % count) for i in range(ends)]),
                cells,
                lax.ppermute(head, axis, [((i + 1) % count, i) for i in range(ends)]),
            ],
            axis=dim,
        )
    return cells


def column_sum(values):
    width = values.shape[-1]
    padding = tuple(((0, 0) for _ in range(values.ndim - 1))) + ((3, 3),)
    padded = jnp.pad(values, padding)
    total = padded[..., 0:width]
    for offset in range(1, 7):
        total = total + padded[..., offset : offset + width]
    return total


def row_sum(values):
    height = values.shape[-2] - 6
    total = values[..., 0:height, :]
    for offset in range(1, 7):
        total = total + values[..., offset : offset + height, :]
    return total


def shards(slc, valid_rows, pair_order):
    per_dev = slc.shape[1]
    band = pair_order.shape[1]
    need = (band + per_dev - 1) // per_dev
    groups = lax.axis_size("date")
    reach = min(need, groups - 1)
    local_idx = jnp.arange(per_dev, dtype=jnp.int32)[:, None] + 1 + pair_order
    slab = slc * valid_rows.astype(jnp.bfloat16)[None, :, :, None]
    padded = with_halo(slab, (("row", 2),), 3)
    pieces = [padded]
    for step in range(1, reach + 1):
        pieces.append(passed_along(padded, "date", -step))
    joined = jnp.concatenate(pieces, axis=1)
    other = jnp.take(joined, local_idx, axis=1).astype(jnp.float32)
    own = joined[:, :per_dev].astype(jnp.float32)
    prod_re = own[0][:, None] * other[0] + own[1][:, None] * other[1]
    prod_im = own[1][:, None] * other[0] - own[0][:, None] * other[1]
    wide = joined.astype(jnp.float32)
    inten = wide[0] * wide[0] + wide[1] * wide[1]
    prod_re, prod_im, inten = (prod_re, prod_im, inten)
    sum_re = row_sum(column_sum(prod_re))
    sum_im = row_sum(column_sum(prod_im))
    inten_sums = row_sum(column_sum(inten))
    first_sum = inten_sums[:per_dev]
    second_sum = jnp.take(inten_sums, local_idx, axis=0)
    magnitude = jnp.sqrt(sum_re * sum_re + sum_im * sum_im)
    scale = 1.0 / jnp.maximum(magnitude, 1.0)
    phase = jnp.stack([sum_re * scale, sum_im * scale]).astype(jnp.bfloat16)
    coher = magnitude / jnp.sqrt(jnp.maximum(first_sum[:, None] * second_sum, 1.0))
    return (phase, coher.astype(jnp.bfloat16))


def solution(mesh):
    placed = (P(None, "date", "row", None), P("date", "row"), P("date", None))
    return jax.shard_map(
        shards,
        mesh=mesh,
        in_specs=placed,
        out_specs=(P(None, "date", None, "row", None), P("date", None, "row", None)),
        check_vma=False,
    )
```

profile of v0, /device:TPU:254, one launch (start us, length us, event | category | flops | bytes accessed | tf_op | source)
XLA Modules:
  0.0 137.3 jit_solution(9390817481064131730)
XLA Ops:
  0.6 0.7 convert_bitcast_fusion
  1.3 1.0 copy_multiply_fusion.3
  2.3 1.7 %collective-permute-start = (bf16[2,1,3,1024]{3,0,2,1:T(2,128)(2,1)S(1)}, bf16[2,1,3,1024]{3,0,2,1:T(2,128)(2,1)S(1)}, u32[]{:S(2)}, u32[]{:S(2)}) collective-permute-start(bf16[2,1,3,1024]{3,0,2,1:T(2,128)(2,1)S(1)} %get-tuple-element.14), channel_id=1, source_target_pairs={{0,1},{2,3},{4,5},{6,7},{8,9},{10,11},{12,13},{14,15},{16,17},{18,... | collective-permute-start | bytes 36872 | tf_op jit(solution)/shard_map/ppermute | solution.py:21
  4.0 1.3 collective-permute-start.1
  5.3 0.7 and_bitcast_fusion
  6.0 0.7 fusion.25
  6.7 0.4 collective-permute-done.1
  7.1 0.1 constant_dynamic-update-slice_fusion.10
  7.2 4.9 %collective-permute-start.11 = (bf16[2,1,22,1024]{3,0,2,1:T(2,128)(2,1)S(1)}, bf16[2,1,22,1024]{3,0,2,1:T(2,128)(2,1)S(1)}, u32[]{:S(2)}, u32[]{:S(2)}) collective-permute-start(bf16[2,1,22,1024]{3,0,2,1:T(2,128)(2,1)S(1)} %get-tuple-element.5), channel_id=1, source_target_pairs={{20,0},{22,2},{24,4},{26,6},{28,8},{30,10},{32,12},{34,14},{36,16}... | collective-permute-start | bytes 270344 | tf_op jit(solution)/shard_map/ppermute | solution.py:10
  12.1 2.5 %collective-permute-start.10 = (bf16[2,1,22,1024]{3,0,2,1:T(2,128)(2,1)S(1)}, bf16[2,1,22,1024]{3,0,2,1:T(2,128)(2,1)S(1)}, u32[]{:S(2)}, u32[]{:S(2)}) collective-permute-start(bf16[2,1,22,1024]{3,0,2,1:T(2,128)(2,1)S(1)} %get-tuple-element.5), channel_id=1, source_target_pairs={{18,0},{20,2},{22,4},{24,6},{26,8},{28,10},{30,12},{32,14},{34,16}... | collective-permute-start | bytes 270344 | tf_op jit(solution)/shard_map/ppermute | solution.py:10
  14.6 2.6 %collective-permute-start.9 = (bf16[2,1,22,1024]{3,0,2,1:T(2,128)(2,1)S(1)}, bf16[2,1,22,1024]{3,0,2,1:T(2,128)(2,1)S(1)}, u32[]{:S(2)}, u32[]{:S(2)}) collective-permute-start(bf16[2,1,22,1024]{3,0,2,1:T(2,128)(2,1)S(1)} %get-tuple-element.5), channel_id=1, source_target_pairs={{16,0},{18,2},{20,4},{22,6},{24,8},{26,10},{28,12},{30,14},{32,16}... | collective-permute-start | bytes 270344 | tf_op jit(solution)/shard_map/ppermute | solution.py:10
  17.2 6.8 %collective-permute-start.8 = (bf16[2,1,22,1024]{3,0,2,1:T(2,128)(2,1)S(1)}, bf16[2,1,22,1024]{3,0,2,1:T(2,128)(2,1)S(1)}, u32[]{:S(2)}, u32[]{:S(2)}) collective-permute-start(bf16[2,1,22,1024]{3,0,2,1:T(2,128)(2,1)S(1)} %get-tuple-element.5), channel_id=1, source_target_pairs={{14,0},{16,2},{18,4},{20,6},{22,8},{24,10},{26,12},{28,14},{30,16}... | collective-permute-start | bytes 270344 | tf_op jit(solution)/shard_map/ppermute | solution.py:10
  24.0 1.9 %collective-permute-start.2 = (bf16[2,1,22,1024]{3,0,2,1:T(2,128)(2,1)S(1)}, bf16[2,1,22,1024]{3,0,2,1:T(2,128)(2,1)S(1)}, u32[]{:S(2)}, u32[]{:S(2)}) collective-permute-start(bf16[2,1,22,1024]{3,0,2,1:T(2,128)(2,1)S(1)} %get-tuple-element.5), channel_id=1, source_target_pairs={{2,0},{4,2},{6,4},{8,6},{10,8},{12,10},{14,12},{16,14},{18,16},{20... | collective-permute-start | bytes 270344 | tf_op jit(solution)/shard_map/ppermute | solution.py:10
  25.9 0.1 fusion.26
  26.1 14.8 %collective-permute-done.2 = bf16[2,1,22,1024]{3,0,2,1:T(2,128)(2,1)S(1)} collective-permute-done((bf16[2,1,22,1024]{3,0,2,1:T(2,128)(2,1)S(1)}, bf16[2,1,22,1024]{3,0,2,1:T(2,128)(2,1)S(1)}, u32[]{:S(2)}, u32[]{:S(2)}) %collective-permute-start.2) | collective-permute-done | bytes 90144 | tf_op jit(solution)/shard_map/ppermute | solution.py:10
  40.9 1.9 %collective-permute-start.3 = (bf16[2,1,22,1024]{3,0,2,1:T(2,128)(2,1)S(1)}, bf16[2,1,22,1024]{3,0,2,1:T(2,128)(2,1)S(1)}, u32[]{:S(2)}, u32[]{:S(2)}) collective-permute-start(bf16[2,1,22,1024]{3,0,2,1:T(2,128)(2,1)S(1)} %get-tuple-element.5), channel_id=1, source_target_pairs={{4,0},{6,2},{8,4},{10,6},{12,8},{14,10},{16,12},{18,14},{20,16},{2... | collective-permute-start | bytes 270344 | tf_op jit(solution)/shard_map/ppermute | solution.py:10
  42.9 10.1 %collective-permute-done.3 = bf16[2,1,22,1024]{3,0,2,1:T(2,128)(2,1)S(1)} collective-permute-done((bf16[2,1,22,1024]{3,0,2,1:T(2,128)(2,1)S(1)}, bf16[2,1,22,1024]{3,0,2,1:T(2,128)(2,1)S(1)}, u32[]{:S(2)}, u32[]{:S(2)}) %collective-permute-start.3) | collective-permute-done | bytes 90144 | tf_op jit(solution)/shard_map/ppermute | solution.py:10
  53.0 1.9 %collective-permute-start.4 = (bf16[2,1,22,1024]{3,0,2,1:T(2,128)(2,1)S(1)}, bf16[2,1,22,1024]{3,0,2,1:T(2,128)(2,1)S(1)}, u32[]{:S(2)}, u32[]{:S(2)}) collective-permute-start(bf16[2,1,22,1024]{3,0,2,1:T(2,128)(2,1)S(1)} %get-tuple-element.5), channel_id=1, source_target_pairs={{6,0},{8,2},{10,4},{12,6},{14,8},{16,10},{18,12},{20,14},{22,16},{... | collective-permute-start | bytes 270344 | tf_op jit(solution)/shard_map/ppermute | solution.py:10
  55.0 8.6 %collective-permute-done.4 = bf16[2,1,22,1024]{3,0,2,1:T(2,128)(2,1)S(1)} collective-permute-done((bf16[2,1,22,1024]{3,0,2,1:T(2,128)(2,1)S(1)}, bf16[2,1,22,1024]{3,0,2,1:T(2,128)(2,1)S(1)}, u32[]{:S(2)}, u32[]{:S(2)}) %collective-permute-start.4) | collective-permute-done | bytes 90144 | tf_op jit(solution)/shard_map/ppermute | solution.py:10
  63.7 1.9 %collective-permute-start.5 = (bf16[2,1,22,1024]{3,0,2,1:T(2,128)(2,1)S(1)}, bf16[2,1,22,1024]{3,0,2,1:T(2,128)(2,1)S(1)}, u32[]{:S(2)}, u32[]{:S(2)}) collective-permute-start(bf16[2,1,22,1024]{3,0,2,1:T(2,128)(2,1)S(1)} %get-tuple-element.5), channel_id=1, source_target_pairs={{8,0},{10,2},{12,4},{14,6},{16,8},{18,10},{20,12},{22,14},{24,16},... | collective-permute-start | bytes 270344 | tf_op jit(solution)/shard_map/ppermute | solution.py:10
  65.6 0.1 constant_dynamic-update-slice_fusion.7
  65.7 8.7 %collective-permute-done.5 = bf16[2,1,22,1024]{3,0,2,1:T(2,128)(2,1)S(1)} collective-permute-done((bf16[2,1,22,1024]{3,0,2,1:T(2,128)(2,1)S(1)}, bf16[2,1,22,1024]{3,0,2,1:T(2,128)(2,1)S(1)}, u32[]{:S(2)}, u32[]{:S(2)}) %collective-permute-start.5) | collective-permute-done | bytes 90144 | tf_op jit(solution)/shard_map/ppermute | solution.py:10
  74.3 1.9 %collective-permute-start.6 = (bf16[2,1,22,1024]{3,0,2,1:T(2,128)(2,1)S(1)}, bf16[2,1,22,1024]{3,0,2,1:T(2,128)(2,1)S(1)}, u32[]{:S(2)}, u32[]{:S(2)}) collective-permute-start(bf16[2,1,22,1024]{3,0,2,1:T(2,128)(2,1)S(1)} %get-tuple-element.5), channel_id=1, source_target_pairs={{10,0},{12,2},{14,4},{16,6},{18,8},{20,10},{22,12},{24,14},{26,16}... | collective-permute-start | bytes 270344 | tf_op jit(solution)/shard_map/ppermute | solution.py:10
  76.3 12.4 %collective-permute-done.6 = bf16[2,1,22,1024]{3,0,2,1:T(2,128)(2,1)S(1)} collective-permute-done((bf16[2,1,22,1024]{3,0,2,1:T(2,128)(2,1)S(1)}, bf16[2,1,22,1024]{3,0,2,1:T(2,128)(2,1)S(1)}, u32[]{:S(2)}, u32[]{:S(2)}) %collective-permute-start.6) | collective-permute-done | bytes 90144 | tf_op jit(solution)/shard_map/ppermute | solution.py:10
  88.7 1.9 %collective-permute-start.7 = (bf16[2,1,22,1024]{3,0,2,1:T(2,128)(2,1)S(1)}, bf16[2,1,22,1024]{3,0,2,1:T(2,128)(2,1)S(1)}, u32[]{:S(2)}, u32[]{:S(2)}) collective-permute-start(bf16[2,1,22,1024]{3,0,2,1:T(2,128)(2,1)S(1)} %get-tuple-element.5), channel_id=1, source_target_pairs={{12,0},{14,2},{16,4},{18,6},{20,8},{22,10},{24,12},{26,14},{28,16}... | collective-permute-start | bytes 270344 | tf_op jit(solution)/shard_map/ppermute | solution.py:10
  90.7 11.0 %collective-permute-done.7 = bf16[2,1,22,1024]{3,0,2,1:T(2,128)(2,1)S(1)} collective-permute-done((bf16[2,1,22,1024]{3,0,2,1:T(2,128)(2,1)S(1)}, bf16[2,1,22,1024]{3,0,2,1:T(2,128)(2,1)S(1)}, u32[]{:S(2)}, u32[]{:S(2)}) %collective-permute-start.7) | collective-permute-done | bytes 90144 | tf_op jit(solution)/shard_map/ppermute | solution.py:10
  101.8 0.1 constant_dynamic-update-slice_fusion.3
  101.9 0.1 constant_dynamic-update-slice_fusion.2
  102.2 0.9 convert_element_type.48
  103.0 3.6 %gather_fusion = bf16[10,2,22,1024]{3,1,2,0:T(2,128)(2,1)} fusion(bf16[2,11,22,1024]{3,0,2,1:T(2,128)(2,1)S(1)} %constant_dynamic-update-slice_fusion, s32[1024]{0:T(1024)S(1)} %pad_clamp_fusion), kind=kCustom, calls=%fused_computation | custom fusion | bytes 1802280 | tf_op jit(solution)/shard_map/jit(_take)/gather | solution.py:61
  106.6 1.3 fusion.6
  108.0 0.2 copy.48
  108.2 1.7 %fusion.5 = f32[11,22,1024]{2,1,0:T(8,128)S(1)} fusion(f32[11,22,1024]{2,1,0:T(8,128)S(1)} %bitcast.47), kind=kLoop, calls=%fused_computation.20 | loop fusion | flops 1486848 | bytes 1982464 | tf_op jit(solution)/shard_map/add | solution.py:36
  109.9 0.4 slice_add_fusion.1
  110.4 0.6 gather_fusion.1
  111.0 0.6 copy-done
  111.5 0.9 fusion.15
  112.4 1.4 %slice_bitcast_fusion = (f32[1,10,22,1024]{3,0,2,1:T(1,128)S(1)}, f32[1,1,10,22,1024]{4,0,3,2,1:T(1,128)S(1)}) fusion(f32[2,1,10,22,1024]{4,0,3,2,1:T(2,128)S(1)} %fusion.15), kind=kLoop, calls=%fused_computation.36 | loop fusion | bytes 3604480 | tf_op jit(solution)/shard_map/squeeze | solution.py:63
  113.8 0.5 fusion.13
  114.3 1.5 %copy_subtract_fusion = f32[1,10,22,1024]{3,0,2,1:T(1,128)S(1)} fusion(f32[1,10,22,1024]{3,2,1,0:T(8,128)S(1)} %get-tuple-element.11, f32[22,1024]{1,0:T(8,128)S(1)} %get-tuple-element.17, f32[2,1,10,22,1024]{4,0,3,2,1:T(2,128)S(1)} %fusion.15), kind=kLoop, calls=%fused_computation.37 | loop fusion | flops 450560 | bytes 2793472 | tf_op jit(solution)/shard_map/sub | solution.py:64
  115.8 11.5 %slice_add_fusion = f32[1,10,22,1024]{3,0,2,1:T(1,128)S(1)} fusion(f32[1,10,22,1024]{3,0,2,1:T(1,128)S(1)} %copy_subtract_fusion), kind=kLoop, calls=%fused_computation.38 | loop fusion | flops 1351680 | bytes 1802240 | tf_op jit(solution)/shard_map/add | solution.py:36
  127.3 1.6 %fusion.12 = f32[1,10,22,1024]{3,2,1,0:T(8,128)S(1)} fusion(f32[1,10,22,1024]{3,2,1,0:T(8,128)S(1)} %get-tuple-element.10), kind=kLoop, calls=%fused_computation.30 | loop fusion | flops 1351680 | bytes 1802240 | tf_op jit(solution)/shard_map/add | solution.py:36
  128.9 2.9 %slice_add_fusion.7 = f32[1,10,16,1024]{3,0,2,1:T(1,128)S(1)} fusion(f32[1,10,22,1024]{3,0,2,1:T(1,128)S(1)} %slice_add_fusion), kind=kLoop, calls=%fused_computation.46 | loop fusion | flops 983040 | bytes 5242880 | tf_op jit(solution)/shard_map/add | solution.py:44
  131.7 1.5 %fusion.20 = (bf16[1,10,16,1024]{3,2,1,0:T(8,128)(2,1)}, f32[1,10,16,1024]{3,2,1,0:T(8,128)S(1)}) fusion(f32[10,16,1024]{2,1,0:T(8,128)S(1)} %gather_fusion.1, f32[16,1024]{1,0:T(8,128)S(1)} %slice_bitcast_fusion.1, pred[10]{0:T(512)(128)(4,1)S(1)} %and_bitcast_fusion, f32[1,10,16,1024]{3,0,2,1:T(1,128)S(1)} %slice_add_fusion.7, ...), kind=kLoop, calls=%fused_computation.64 | loop fusion | flops 2293760 | bytes 6946826 | tf_op jit(solution)/shard_map/convert_element_type | solution.py:77
  133.2 0.3 fusion.24
  133.5 2.7 %fusion.21 = bf16[1,10,16,1024]{3,0,2,1:T(2,128)(2,1)S(1)} fusion(f32[1,10,16,1024]{3,2,1,0:T(8,128)S(1)} %get-tuple-element.9, f32[1,10,22,1024]{3,0,2,1:T(1,128)S(1)} %slice_add_fusion), kind=kLoop, calls=%fused_computation.66 | loop fusion | flops 1310720 | bytes 5570560 | tf_op jit(solution)/shard_map/convert.2
  136.3 0.1 copy.49
  136.4 0.9 pad_maximum_fusion
  (17 shorter events, 0.6 us)
Async XLA Ops:
  2.3 4.4 %collective-permute-start = (bf16[2,1,3,1024]{3,0,2,1:T(2,128)(2,1)S(1)}, bf16[2,1,3,1024]{3,0,2,1:T(2,128)(2,1)S(1)}, u32[]{:S(2)}, u32[]{:S(2)}) collective-permute-start(bf16[2,1,3,1024]{3,0,2,1:T(2,128)(2,1)S(1)} %get-tuple-element.14), channel_id=1, source_target_pairs={{0,1},{2,3},{4,5},{6,7},{8,9},{10,11},{12,13},{14,15},{16,17},{18,... | collective-permute-start | bytes 36872 | tf_op jit(solution)/shard_map/ppermute | solution.py:21
  4.0 3.1 %collective-permute-start.1 = (bf16[2,1,3,1024]{3,0,2,1:T(2,128)(2,1)S(1)}, bf16[2,1,3,1024]{3,0,2,1:T(2,128)(2,1)S(1)}, u32[]{:S(2)}, u32[]{:S(2)}) collective-permute-start(bf16[2,1,3,1024]{3,0,2,1:T(2,128)(2,1)S(1)} %get-tuple-element.15), channel_id=1, source_target_pairs={{1,0},{3,2},{5,4},{7,6},{9,8},{11,10},{13,12},{15,14},{17,16},{19,... | collective-permute-start | bytes 36872 | tf_op jit(solution)/shard_map/ppermute | solution.py:23
  7.2 94.9 %collective-permute-start.11 = (bf16[2,1,22,1024]{3,0,2,1:T(2,128)(2,1)S(1)}, bf16[2,1,22,1024]{3,0,2,1:T(2,128)(2,1)S(1)}, u32[]{:S(2)}, u32[]{:S(2)}) collective-permute-start(bf16[2,1,22,1024]{3,0,2,1:T(2,128)(2,1)S(1)} %get-tuple-element.5), channel_id=1, source_target_pairs={{20,0},{22,2},{24,4},{26,6},{28,8},{30,10},{32,12},{34,14},{36,16}... | collective-permute-start | bytes 270344 | tf_op jit(solution)/shard_map/ppermute | solution.py:10
  12.1 89.9 %collective-permute-start.10 = (bf16[2,1,22,1024]{3,0,2,1:T(2,128)(2,1)S(1)}, bf16[2,1,22,1024]{3,0,2,1:T(2,128)(2,1)S(1)}, u32[]{:S(2)}, u32[]{:S(2)}) collective-permute-start(bf16[2,1,22,1024]{3,0,2,1:T(2,128)(2,1)S(1)} %get-tuple-element.5), channel_id=1, source_target_pairs={{18,0},{20,2},{22,4},{24,6},{26,8},{28,10},{30,12},{32,14},{34,16}... | collective-permute-start | bytes 270344 | tf_op jit(solution)/shard_map/ppermute | solution.py:10
  14.6 87.3 %collective-permute-start.9 = (bf16[2,1,22,1024]{3,0,2,1:T(2,128)(2,1)S(1)}, bf16[2,1,22,1024]{3,0,2,1:T(2,128)(2,1)S(1)}, u32[]{:S(2)}, u32[]{:S(2)}) collective-permute-start(bf16[2,1,22,1024]{3,0,2,1:T(2,128)(2,1)S(1)} %get-tuple-element.5), channel_id=1, source_target_pairs={{16,0},{18,2},{20,4},{22,6},{24,8},{26,10},{28,12},{30,14},{32,16}... | collective-permute-start | bytes 270344 | tf_op jit(solution)/shard_map/ppermute | solution.py:10
  17.2 84.6 %collective-permute-start.8 = (bf16[2,1,22,1024]{3,0,2,1:T(2,128)(2,1)S(1)}, bf16[2,1,22,1024]{3,0,2,1:T(2,128)(2,1)S(1)}, u32[]{:S(2)}, u32[]{:S(2)}) collective-permute-start(bf16[2,1,22,1024]{3,0,2,1:T(2,128)(2,1)S(1)} %get-tuple-element.5), channel_id=1, source_target_pairs={{14,0},{16,2},{18,4},{20,6},{22,8},{24,10},{26,12},{28,14},{30,16}... | collective-permute-start | bytes 270344 | tf_op jit(solution)/shard_map/ppermute | solution.py:10
  24.0 16.9 %collective-permute-start.2 = (bf16[2,1,22,1024]{3,0,2,1:T(2,128)(2,1)S(1)}, bf16[2,1,22,1024]{3,0,2,1:T(2,128)(2,1)S(1)}, u32[]{:S(2)}, u32[]{:S(2)}) collective-permute-start(bf16[2,1,22,1024]{3,0,2,1:T(2,128)(2,1)S(1)} %get-tuple-element.5), channel_id=1, source_target_pairs={{2,0},{4,2},{6,4},{8,6},{10,8},{12,10},{14,12},{16,14},{18,16},{20... | collective-permute-start | bytes 270344 | tf_op jit(solution)/shard_map/ppermute | solution.py:10
  40.9 12.1 %collective-permute-start.3 = (bf16[2,1,22,1024]{3,0,2,1:T(2,128)(2,1)S(1)}, bf16[2,1,22,1024]{3,0,2,1:T(2,128)(2,1)S(1)}, u32[]{:S(2)}, u32[]{:S(2)}) collective-permute-start(bf16[2,1,22,1024]{3,0,2,1:T(2,128)(2,1)S(1)} %get-tuple-element.5), channel_id=1, source_target_pairs={{4,0},{6,2},{8,4},{10,6},{12,8},{14,10},{16,12},{18,14},{20,16},{2... | collective-permute-start | bytes 270344 | tf_op jit(solution)/shard_map/ppermute | solution.py:10
  53.0 10.6 %collective-permute-start.4 = (bf16[2,1,22,1024]{3,0,2,1:T(2,128)(2,1)S(1)}, bf16[2,1,22,1024]{3,0,2,1:T(2,128)(2,1)S(1)}, u32[]{:S(2)}, u32[]{:S(2)}) collective-permute-start(bf16[2,1,22,1024]{3,0,2,1:T(2,128)(2,1)S(1)} %get-tuple-element.5), channel_id=1, source_target_pairs={{6,0},{8,2},{10,4},{12,6},{14,8},{16,10},{18,12},{20,14},{22,16},{... | collective-permute-start | bytes 270344 | tf_op jit(solution)/shard_map/ppermute | solution.py:10
  63.7 10.6 %collective-permute-start.5 = (bf16[2,1,22,1024]{3,0,2,1:T(2,128)(2,1)S(1)}, bf16[2,1,22,1024]{3,0,2,1:T(2,128)(2,1)S(1)}, u32[]{:S(2)}, u32[]{:S(2)}) collective-permute-start(bf16[2,1,22,1024]{3,0,2,1:T(2,128)(2,1)S(1)} %get-tuple-element.5), channel_id=1, source_target_pairs={{8,0},{10,2},{12,4},{14,6},{16,8},{18,10},{20,12},{22,14},{24,16},... | collective-permute-start | bytes 270344 | tf_op jit(solution)/shard_map/ppermute | solution.py:10
  74.3 14.4 %collective-permute-start.6 = (bf16[2,1,22,1024]{3,0,2,1:T(2,128)(2,1)S(1)}, bf16[2,1,22,1024]{3,0,2,1:T(2,128)(2,1)S(1)}, u32[]{:S(2)}, u32[]{:S(2)}) collective-permute-start(bf16[2,1,22,1024]{3,0,2,1:T(2,128)(2,1)S(1)} %get-tuple-element.5), channel_id=1, source_target_pairs={{10,0},{12,2},{14,4},{16,6},{18,8},{20,10},{22,12},{24,14},{26,16}... | collective-permute-start | bytes 270344 | tf_op jit(solution)/shard_map/ppermute | solution.py:10
  88.7 13.0 %collective-permute-start.7 = (bf16[2,1,22,1024]{3,0,2,1:T(2,128)(2,1)S(1)}, bf16[2,1,22,1024]{3,0,2,1:T(2,128)(2,1)S(1)}, u32[]{:S(2)}, u32[]{:S(2)}) collective-permute-start(bf16[2,1,22,1024]{3,0,2,1:T(2,128)(2,1)S(1)} %get-tuple-element.5), channel_id=1, source_target_pairs={{12,0},{14,2},{16,4},{18,6},{20,8},{22,10},{24,12},{26,14},{28,16}... | collective-permute-start | bytes 270344 | tf_op jit(solution)/shard_map/ppermute | solution.py:10
  110.4 1.2 copy-start
where the time goes:
time: 138 us; the launch traced here: 137 us
  waiting for transfers between devices  66.1 us (48%)
  other arithmetic  31.6 us (23%)
  starting transfers between devices  31.2 us (23%)
  local copies, waits for them, and re-layouts  7.4 us (5%)
    ppermute x10, waiting for transfers between devices, passed_along(): return lax.ppermute(shard, axis, pairs)  65.7 us
    ppermute x10, starting transfers between devices, passed_along(): return lax.ppermute(shard, axis, pairs)  28.2 us
    add x3, other arithmetic, column_sum(): total = total + padded[..., offset:offset + width]  14.8 us
    gather x1, local copies, waits for them, and re-layouts, shards(): other = jnp.take(joined, local_idx, axis=1).astype(jnp.float32)  3.59 us
    add x2, other arithmetic, row_sum(): total = total + values[..., offset:offset + height, :]  3.3 us
  transfers between devices with their start and end apart: 12, of which 7 were waited for; matrix products, arithmetic and copies ran while one was open for 2% of the time, Pallas kernels for 0%

commit v1 on v0

v1 whole, which is shorter than its diff:
```python
import jax
import jax.numpy as jnp
from jax import lax
from jax.experimental import pallas as pl
from jax.experimental.pallas import tpu as pltpu
from jax.sharding import PartitionSpec as P

GROUP = 8
HALO = 3
BLOCK = 128


def shifted(shard, by):
    length = lax.axis_size("date")
    return lax.ppermute(shard, "date", [(i, i - by) for i in range(by, length)])


def vertical(rows):
    count = rows.shape[0] - 6
    two = rows[:-1] + rows[1:]
    four = two[:-2] + two[2:]
    return four[:count] + two[4 : 4 + count] + rows[6 : 6 + count]


def moved(x, by, before, after):
    lane = lax.broadcasted_iota(jnp.int32, x.shape, 2)
    if by > 0:
        near = jnp.concatenate([before, x[:-1]], axis=0)
        mixed = jnp.where(lane >= BLOCK - by, near, x)
    else:
        near = jnp.concatenate([x[1:], after], axis=0)
        mixed = jnp.where(lane < -by, near, x)
    return pltpu.roll(mixed, by % BLOCK, 2)


def horizontal(x):
    zero = jnp.zeros_like(x[:1])
    lane = lax.broadcasted_iota(jnp.int32, zero.shape, 2)
    three = x + moved(x, 1, zero, zero) + moved(x, -1, zero, zero)
    before = jnp.where(lane == BLOCK - 1, pltpu.roll(x[:1], BLOCK - 1, 2), zero)
    after = jnp.where(lane == 0, pltpu.roll(x[-1:], 1, 2), zero)
    return x + moved(three, 2, before, after) + moved(three, -2, before, after)


def kernel(order, place, own, near, nine, ten, phase, coher, slots, padded, sums, first):
    own_rows, cells = own.shape[0], 8
    height = own_rows - HALO
    blocks = phase.shape[-1] // BLOCK
    core, rank = place[0], place[1]
    start = HALO * (1 - core)
    band = order.shape[1]
    for j in range(band):
        slots[order[0, j]] = j
    padded[...] = jnp.zeros_like(padded)

    def box_to(index, values):
        padded[index, pl.ds(start, own_rows)] = values

    def columns(index):
        chunk = 4
        for base in range(0, height, chunk):
            got = vertical(padded[index, base : base + chunk + 6])
            for i in range(chunk):
                sums[index, pl.ds(base + i, blocks, stride=height), :] = got[i]

    def summed(index, half):
        x = sums[index].reshape(blocks, height, BLOCK)[:, half * 8 : half * 8 + 8]
        return horizontal(x)

    def intensity(pair):
        return pair[:, :cells] * pair[:, :cells] + pair[:, cells:] * pair[:, cells:]

    mine = own[...].astype(jnp.float32)
    box_to(2, intensity(mine))
    columns(2)
    for half in range(height // 8):
        first[:, half * 8 : half * 8 + 8] = summed(2, half)

    def one(other, offset):
        slot = slots[offset - 1]
        a = own[...].astype(jnp.float32)
        b = other.astype(jnp.float32)
        a0, a1, b0, b1 = a[:, :cells], a[:, cells:], b[:, :cells], b[:, cells:]
        box_to(0, a0 * b0 + a1 * b1)
        box_to(1, a1 * b0 - a0 * b1)
        box_to(2, b0 * b0 + b1 * b1)
        for index in range(3):
            columns(index)
        res = [[], [], []]
        for half in range(height // 8):
            re, im, second = (summed(index, half) for index in range(3))
            power = re * re + im * im
            scale = lax.rsqrt(jnp.maximum(power, 1.0))
            both = first[:, half * 8 : half * 8 + 8] * second
            co = jnp.sqrt(power) * lax.rsqrt(jnp.maximum(both, 1.0))
            for kept, value in zip(res, (re * scale, im * scale, co)):
                kept.append(value)
        re, im, co = (jnp.concatenate(kept, axis=1).astype(jnp.bfloat16) for kept in res)
        for b in range(blocks):
            at = slice(b * BLOCK, (b + 1) * BLOCK)
            phase[0, slot, :, at] = re[b]
            phase[1, slot, :, at] = im[b]
            coher[slot, :, at] = co[b]

    def step(p, carry):
        offset = lax.rem(p - rank + GROUP - 1, GROUP) + 1
        one(near[p], offset)
        return carry

    lax.fori_loop(0, GROUP, step, 0)
    one(nine[...], 9)
    one(ten[...], 10)


def shards(slc, valid_rows, pair_order):
    _, _, height, width = slc.shape
    band = pair_order.shape[1]
    blocks = width // BLOCK
    cells = 2 * blocks
    core = lax.axis_index("row")
    rank = lax.rem(lax.axis_index("date"), GROUP)
    slab = slc[:, 0] * valid_rows.astype(jnp.bfloat16)[0][None, :, None]
    slab = slab.reshape(2, height, blocks, BLOCK).transpose(1, 0, 2, 3).reshape(height, cells, BLOCK)
    edge = lax.dynamic_slice_in_dim(slab, (height - HALO) * (1 - core), HALO, axis=0)
    halo = lax.ppermute(edge, "row", [(0, 1), (1, 0)])
    own = jnp.where(
        core == 0,
        jnp.concatenate([slab, halo], axis=0),
        jnp.concatenate([halo, slab], axis=0),
    )
    eight = shifted(own, 8)
    nine = shifted(own, 9)
    ten = shifted(own, 10)
    members = jnp.arange(GROUP)[:, None, None, None]
    given = jnp.where(members < rank, own[None], eight[None])
    length = lax.axis_size("date")
    groups = [list(range(g, g + GROUP)) for g in range(0, length, GROUP)]
    near = lax.all_to_all(given, "date", 0, 0, axis_index_groups=groups, tiled=True)
    place = jnp.stack([core, rank]).astype(jnp.int32)
    rows = height + HALO
    whole = pl.BlockSpec(memory_space=pltpu.VMEM)
    scalars = pl.BlockSpec(memory_space=pltpu.SMEM)
    phase, coher = pl.pallas_call(
        kernel,
        out_shape=(
            jax.ShapeDtypeStruct((2, band, height, width), jnp.bfloat16),
            jax.ShapeDtypeStruct((band, height, width), jnp.bfloat16),
        ),
        in_specs=[scalars, scalars, whole, whole, whole, whole],
        out_specs=(whole, whole),
        scratch_shapes=[
            pltpu.SMEM((band,), jnp.int32),
            pltpu.VMEM((3, height + 2 * HALO, blocks, BLOCK), jnp.float32),
            pltpu.VMEM((3, blocks * height, BLOCK), jnp.float32),
            pltpu.VMEM((blocks, height, BLOCK), jnp.float32),
        ],
        compiler_params=pltpu.CompilerParams(vmem_limit_bytes=24 << 20),
        cost_estimate=pl.CostEstimate(flops=20 << 20, bytes_accessed=3 << 20, transcendentals=1 << 19),
    )(pair_order, place, own, near, nine, ten)
    return phase[:, None], coher[None]


def solution(mesh):
    placed = (P(None, "date", "row", None), P("date", "row"), P("date", None))
    return jax.shard_map(
        shards,
        mesh=mesh,
        in_specs=placed,
        out_specs=(P(None, "date", None, "row", None), P("date", None, "row", None)),
        check_vma=False,
    )
```

time: 138 us -> 50.9 us (0.37)
  the two profiles are of different devices: /device:TPU:254 before, /device:TPU:246 now
where the time goes in v1:
time: 50.9 us; the launch traced here: 50.6 us
  waiting for transfers between devices  25.8 us (51%)
  starting transfers between devices  14.6 us (29%)
  Pallas kernels  6.88 us (14%)
  local copies, waits for them, and re-layouts  1.51 us (3%)
  other arithmetic  1.12 us (2%)
  between operations  0.73 us (1%)
    ppermute x3, waiting for transfers between devices, shifted(): return lax.ppermute(shard, 'date', [(i, i - by) for i in range(by, length)])  24.6 us
    ppermute x3, starting transfers between devices, shifted(): return lax.ppermute(shard, 'date', [(i, i - by) for i in range(by, length)])  7.94 us
    pallas_call x1, Pallas kernels, shards(): pl.pallas_call(kernel, out_shape=(jax.ShapeDtypeStruct((2, band, height,...  6.88 us
    all_to_all x1, starting transfers between devices, shards(): lax.all_to_all(given, 'date', 0, 0, axis_index_groups=groups, tiled=True)  4.77 us
    ppermute x1, starting transfers between devices, shards(): halo = lax.ppermute(edge, 'row', [(0, 1), (1, 0)])  1.92 us
    unnamed x5, local copies, waits for them, and re-layouts  1.5 us
    ppermute x1, waiting for transfers between devices, shards(): halo = lax.ppermute(edge, 'row', [(0, 1), (1, 0)])  1.13 us
  transfers between devices with their start and end apart: 5, of which 4 were waited for; matrix products, arithmetic and copies ran while one was open for 0% of the time, Pallas kernels for 0%

profile of v1, /device:TPU:246, one launch (start us, length us, event | category | flops | bytes accessed | tf_op | source)
XLA Modules:
  0.0 50.6 jit_solution(17237702160543386748)
XLA Ops:
  0.6 0.0 copy-start.1
  0.6 0.6 %copy-done.1 = s32[1,16]{1,0:T(1,128)S(1)} copy-done((s32[1,16]{1,0:T(1,128)S(1)}, s32[1,16]{1,0:T(1,128)}, u32[]{:S(2)}) %copy-start.1) | copy-done | bytes 88
  1.3 0.8 %copy.7 = bf16[4,8,8,128]{3,2,1,0:T(8,128)(2,1)S(1)} copy(bf16[4,8,8,128]{3,1,2,0:T(8,128)(2,1)} %bitcast.22) | data formatting | bytes 131072
  2.2 0.1 fusion
  2.3 1.9 %collective-permute-start = (bf16[3,16,128]{2,1,0:T(8,128)(2,1)S(1)}, bf16[3,16,128]{2,1,0:T(8,128)(2,1)S(1)}, u32[]{:S(2)}, u32[]{:S(2)}) collective-permute-start(bf16[3,16,128]{2,1,0:T(8,128)(2,1)S(1)} %constant_dynamic-slice_fusion), channel_id=1, source_target_pairs={{0,1},{1,0},{2,3},{3,2},{4,5},{5,4},{6,7},{7,6},{8,9},{9,8},{10,11... | collective-permute-start | bytes 36872 | tf_op jit(solution)/shard_map/ppermute | solution.py:125
  4.2 1.1 %collective-permute-done = bf16[3,16,128]{2,1,0:T(8,128)(2,1)S(1)} collective-permute-done((bf16[3,16,128]{2,1,0:T(8,128)(2,1)S(1)}, bf16[3,16,128]{2,1,0:T(8,128)(2,1)S(1)}, u32[]{:S(2)}, u32[]{:S(2)}) %collective-permute-start) | collective-permute-done | bytes 12320 | tf_op jit(solution)/shard_map/ppermute | solution.py:125
  5.3 4.0 %collective-permute-start.1 = (bf16[19,16,128]{2,1,0:T(8,128)(2,1)S(1)}, bf16[19,16,128]{2,1,0:T(8,128)(2,1)S(1)}, u32[]{:S(2)}, u32[]{:S(2)}) collective-permute-start(bf16[19,16,128]{2,1,0:T(8,128)(2,1)S(1)} %maximum_select_fusion.own), channel_id=1, source_target_pairs={{16,0},{18,2},{20,4},{22,6},{24,8},{26,10},{28,12},{30,14},{32,16}... | collective-permute-start | bytes 233480 | tf_op jit(solution)/shard_map/ppermute | solution.py:15
  9.4 8.1 %collective-permute-done.1 = bf16[19,16,128]{2,1,0:T(8,128)(2,1)S(1)} collective-permute-done((bf16[19,16,128]{2,1,0:T(8,128)(2,1)S(1)}, bf16[19,16,128]{2,1,0:T(8,128)(2,1)S(1)}, u32[]{:S(2)}, u32[]{:S(2)}) %collective-permute-start.1) | collective-permute-done | bytes 77856 | tf_op jit(solution)/shard_map/ppermute | solution.py:15
  17.6 0.9 %broadcast_select_fusion = bf16[8,19,16,128]{3,2,1,0:T(8,128)(2,1)} fusion(pred[8]{0:T(512)(128)(4,1)S(1)} %iota_compare_fusion, bf16[19,16,128]{2,1,0:T(8,128)(2,1)S(1)} %collective-permute-done.1, bf16[19,16,128]{2,1,0:T(8,128)(2,1)S(1)} %maximum_select_fusion.own), kind=kLoop, calls=%fused_computation | loop fusion | flops 311296 | bytes 778248 | tf_op jit(solution)/shard_map/jit(_where)/select_n | solution.py:135
  18.5 4.8 %all-to-all-start = ((bf16[8,19,16,128]{3,2,1,0:T(8,128)(2,1)}), bf16[8,19,16,128]{3,2,1,0:T(8,128)(2,1)S(1)}, u32[]{:S(2)}, u32[]{:S(2)}) async-start(bf16[8,19,16,128]{3,2,1,0:T(8,128)(2,1)} %broadcast_select_fusion), calls=%async_computation | async-start | bytes 1245184 | tf_op jit(solution)/shard_map/all_to_all | solution.py:138
  23.3 1.9 %collective-permute-start.3 = (bf16[19,16,128]{2,1,0:T(8,128)(2,1)S(1)}, bf16[19,16,128]{2,1,0:T(8,128)(2,1)S(1)}, u32[]{:S(2)}, u32[]{:S(2)}) collective-permute-start(bf16[19,16,128]{2,1,0:T(8,128)(2,1)S(1)} %maximum_select_fusion.own), channel_id=1, source_target_pairs={{20,0},{22,2},{24,4},{26,6},{28,8},{30,10},{32,12},{34,14},{36,16}... | collective-permute-start | bytes 233480 | tf_op jit(solution)/shard_map/ppermute | solution.py:15
  25.2 2.0 %collective-permute-start.2 = (bf16[19,16,128]{2,1,0:T(8,128)(2,1)S(1)}, bf16[19,16,128]{2,1,0:T(8,128)(2,1)S(1)}, u32[]{:S(2)}, u32[]{:S(2)}) collective-permute-start(bf16[19,16,128]{2,1,0:T(8,128)(2,1)S(1)} %maximum_select_fusion.own), channel_id=1, source_target_pairs={{18,0},{20,2},{22,4},{24,6},{26,8},{28,10},{30,12},{32,14},{34,16}... | collective-permute-start | bytes 233480 | tf_op jit(solution)/shard_map/ppermute | solution.py:15
  27.2 0.0 copy-start
  27.2 0.1 pad_add_fusion.place
  27.3 14.4 %collective-permute-done.3.ten = bf16[19,16,128]{2,1,0:T(8,128)(2,1)S(1)} collective-permute-done((bf16[19,16,128]{2,1,0:T(8,128)(2,1)S(1)}, bf16[19,16,128]{2,1,0:T(8,128)(2,1)S(1)}, u32[]{:S(2)}, u32[]{:S(2)}) %collective-permute-start.3) | collective-permute-done | bytes 77856 | tf_op jit(solution)/shard_map/ppermute | solution.py:15
  41.7 2.1 %collective-permute-done.2.nine = bf16[19,16,128]{2,1,0:T(8,128)(2,1)S(1)} collective-permute-done((bf16[19,16,128]{2,1,0:T(8,128)(2,1)S(1)}, bf16[19,16,128]{2,1,0:T(8,128)(2,1)S(1)}, u32[]{:S(2)}, u32[]{:S(2)}) %collective-permute-start.2) | collective-permute-done | bytes 77856 | tf_op jit(solution)/shard_map/ppermute | solution.py:15
  43.7 0.0 all-to-all-done.near
  43.8 0.0 copy-done
  43.8 6.9 %shard_map.50 = (bf16[2,10,16,1024]{3,2,1,0:T(8,128)(2,1)}, bf16[10,16,1024]{2,1,0:T(8,128)(2,1)}) custom-call(s32[1,10]{1,0:T(1,128)S(1)} %copy-done, s32[2]{0:T(128)S(1)} %pad_add_fusion.place, bf16[19,16,128]{2,1,0:T(8,128)(2,1)S(1)} %maximum_select_fusion.own, bf16[8,19,16,128]{3,2,1,0:T(8,128)(2,1)S(1)} %all-to-all-done.near, ...), custom_call_target="tpu_custom_call" | custom-call | flops 20971520 | bytes 3145728 | tf_op jit(solution)/shard_map/pallas_call | solution.py:143
  (4 shorter events, 0.0 us)
Async XLA Ops:
  0.6 0.7 %copy-start.1 = (s32[1,16]{1,0:T(1,128)S(1)}, s32[1,16]{1,0:T(1,128)}, u32[]{:S(2)}) copy-start(s32[1,16]{1,0:T(1,128)} %param.4) | copy-start | bytes 196
  2.3 3.1 %collective-permute-start = (bf16[3,16,128]{2,1,0:T(8,128)(2,1)S(1)}, bf16[3,16,128]{2,1,0:T(8,128)(2,1)S(1)}, u32[]{:S(2)}, u32[]{:S(2)}) collective-permute-start(bf16[3,16,128]{2,1,0:T(8,128)(2,1)S(1)} %constant_dynamic-slice_fusion), channel_id=1, source_target_pairs={{0,1},{1,0},{2,3},{3,2},{4,5},{5,4},{6,7},{7,6},{8,9},{9,8},{10,11... | collective-permute-start | bytes 36872 | tf_op jit(solution)/shard_map/ppermute | solution.py:125
  5.3 12.2 %collective-permute-start.1 = (bf16[19,16,128]{2,1,0:T(8,128)(2,1)S(1)}, bf16[19,16,128]{2,1,0:T(8,128)(2,1)S(1)}, u32[]{:S(2)}, u32[]{:S(2)}) collective-permute-start(bf16[19,16,128]{2,1,0:T(8,128)(2,1)S(1)} %maximum_select_fusion.own), channel_id=1, source_target_pairs={{16,0},{18,2},{20,4},{22,6},{24,8},{26,10},{28,12},{30,14},{32,16}... | collective-permute-start | bytes 233480 | tf_op jit(solution)/shard_map/ppermute | solution.py:15
  18.5 25.3 %all-to-all-start = ((bf16[8,19,16,128]{3,2,1,0:T(8,128)(2,1)}), bf16[8,19,16,128]{3,2,1,0:T(8,128)(2,1)S(1)}, u32[]{:S(2)}, u32[]{:S(2)}) async-start(bf16[8,19,16,128]{3,2,1,0:T(8,128)(2,1)} %broadcast_select_fusion), calls=%async_computation | async-start | bytes 1245184 | tf_op jit(solution)/shard_map/all_to_all | solution.py:138
  23.3 18.4 %collective-permute-start.3 = (bf16[19,16,128]{2,1,0:T(8,128)(2,1)S(1)}, bf16[19,16,128]{2,1,0:T(8,128)(2,1)S(1)}, u32[]{:S(2)}, u32[]{:S(2)}) collective-permute-start(bf16[19,16,128]{2,1,0:T(8,128)(2,1)S(1)} %maximum_select_fusion.own), channel_id=1, source_target_pairs={{20,0},{22,2},{24,4},{26,6},{28,8},{30,10},{32,12},{34,14},{36,16}... | collective-permute-start | bytes 233480 | tf_op jit(solution)/shard_map/ppermute | solution.py:15
  25.2 18.6 %collective-permute-start.2 = (bf16[19,16,128]{2,1,0:T(8,128)(2,1)S(1)}, bf16[19,16,128]{2,1,0:T(8,128)(2,1)S(1)}, u32[]{:S(2)}, u32[]{:S(2)}) collective-permute-start(bf16[19,16,128]{2,1,0:T(8,128)(2,1)S(1)} %maximum_select_fusion.own), channel_id=1, source_target_pairs={{18,0},{20,2},{22,4},{24,6},{26,8},{28,10},{30,12},{32,14},{34,16}... | collective-permute-start | bytes 233480 | tf_op jit(solution)/shard_map/ppermute | solution.py:15
  27.2 16.6 %copy-start = (s32[1,10]{1,0:T(1,128)S(1)}, s32[1,10]{1,0:T(1,128)}, u32[]{:S(2)}) copy-start(s32[1,10]{1,0:T(1,128)} %order.1) | copy-start | bytes 124

commit v2 on v0

v2 whole, which is shorter than its diff:
```python
import jax
import jax.numpy as jnp
from jax import lax
from jax.experimental import pallas as pl
from jax.experimental.pallas import tpu as pltpu
from jax.sharding import PartitionSpec as P

GROUP = 8
HALO = 3
BLOCK = 128
TINY = 1.1754944e-38
WHOLE = pl.BlockSpec(memory_space=pltpu.VMEM)
SCALARS = pl.BlockSpec(memory_space=pltpu.SMEM)
AWAY = pl.BlockSpec(memory_space=pl.ANY)


class Column:
    def __init__(self):
        self.rows, self.two, self.four = [], [], []

    def feed(self, row):
        rows, two, four = self.rows, self.two, self.four
        rows.append(row)
        at = len(rows) - 1
        if at >= 1:
            two.append(rows[at - 1] + row)
        if at >= 3:
            four.append(two[at - 3] + two[at - 1])
        out = at - HALO
        if out < 0:
            return None
        if out == 0:
            return four[0]
        if out == 1:
            return four[0] + rows[4]
        if out == 2:
            return four[0] + two[4]
        return four[out - 3] + two[out + 1] + row


def band_matrix(ref):
    shape = (BLOCK, 2 * BLOCK)
    source = lax.broadcasted_iota(jnp.int32, shape, 0)
    target = lax.broadcasted_iota(jnp.int32, shape, 1)
    gap = jnp.where(target < BLOCK, jnp.abs(target - source), BLOCK - jnp.abs(target - BLOCK - source))
    ones = (gap <= HALO).astype(jnp.float32).astype(jnp.bfloat16)
    for part in range(3):
        ref[part * BLOCK : (part + 1) * BLOCK, :] = ones


def horizontal(x, band):
    count, blocks, height, _ = x.shape
    x = x.reshape(count * blocks * height, BLOCK)
    high = x.astype(jnp.bfloat16)
    rest = x - high.astype(jnp.float32)
    middle = rest.astype(jnp.bfloat16)
    low = (rest - middle.astype(jnp.float32)).astype(jnp.bfloat16)
    parts = jnp.concatenate([high, middle, low], axis=1)
    got = jnp.dot(parts, band, preferred_element_type=jnp.float32)
    got = got.reshape(count, blocks, height, 2 * BLOCK)
    inside, beside = got[..., :BLOCK], got[..., BLOCK:]
    zero = jnp.zeros_like(beside[:, :1])
    before = jnp.concatenate([zero, beside[:, :-1]], axis=1)
    after = jnp.concatenate([beside[:, 1:], zero], axis=1)
    lane = lax.broadcasted_iota(jnp.int32, beside.shape, 3)
    return inside + jnp.where(lane < BLOCK // 2, before, after)


class Pairs:
    def __init__(self, order, place, own, phase, coher, slots, mine, band, staged, sems):
        self.core = place[0]
        self.phase, self.coher = phase, coher
        self.slots, self.mine, self.band, self.staged, self.sems = slots, mine, band, staged, sems
        self.rows, self.cells = own.shape[0], own.shape[1] // 2
        self.height, self.blocks = self.rows - HALO, own.shape[1] // 2
        for j in range(order.shape[1]):
            slots[order[0, j]] = j
        for row in range(self.rows):
            mine[row] = own[row].astype(jnp.float32)
        band_matrix(band)

    def store(self, sums, index, row, value):
        if value is not None:
            out = row - HALO
            spot = out + self.core * (self.height - 1 - 2 * out)
            sums[index, pl.ds(spot, self.blocks, stride=self.height), :] = value

    def boxes(self, sums, count):
        x = sums[:count].reshape(count, self.blocks, self.height, BLOCK)
        return horizontal(x, self.band[...])

    def own_intensity(self, sums, first):
        column = Column()
        for row in range(self.rows):
            a0, a1 = self.mine[row, : self.cells], self.mine[row, self.cells :]
            self.store(sums, 0, row, column.feed(a0 * a0 + a1 * a1))
        first[...] = self.boxes(sums, 1)[0]

    def copies(self, turn, slot):
        kept, sems = self.staged.at[turn], self.sems.at[turn]
        return (
            pltpu.make_async_copy(kept.at[0:2], self.phase.at[:, slot], sems.at[0]),
            pltpu.make_async_copy(kept.at[2], self.coher.at[slot], sems.at[1]),
        )

    def one(self, other, offset, turn, sums, first):
        slot = self.slots[offset - 1]
        columns = [Column() for _ in range(3)]
        for row in range(self.rows):
            a0, a1 = self.mine[row, : self.cells], self.mine[row, self.cells :]
            b = other[row].astype(jnp.float32)
            b0, b1 = b[: self.cells], b[self.cells :]
            values = (a0 * b0 + a1 * b1, a1 * b0 - a0 * b1, b0 * b0 + b1 * b1)
            for index, value in enumerate(values):
                self.store(sums, index, row, columns[index].feed(value))
        re, im, second = self.boxes(sums, 3)
        power = re * re + im * im
        inverse = lax.rsqrt(jnp.maximum(power, TINY))
        scale = jnp.minimum(inverse, 1.0)
        both = first[...] * second
        co = power * inverse * lax.rsqrt(jnp.maximum(both, 1.0))
        for index, value in enumerate((re * scale, im * scale, co)):
            value = value.astype(jnp.bfloat16)
            for b in range(self.blocks):
                self.staged[turn, index, :, b * BLOCK : (b + 1) * BLOCK] = value[b]
        for copy in self.copies(turn, slot):
            copy.start()

    def finish(self, turns):
        for turn in range(turns):
            for copy in self.copies(turn, 0):
                copy.wait()


def first_kernel(order, place, own, eight, phase, coher, first, slots, mine, band, staged, sems, *sums):
    pairs = Pairs(order, place, own, phase, coher, slots, mine, band, staged, sems)
    pairs.own_intensity(sums[1], first)
    pairs.one(eight, GROUP, 0, sums[0], first)
    pairs.finish(1)


def near_kernel(order, place, own, near, first, _p, _c, phase, coher, slots, mine, band, staged, sems, *sums):
    pairs = Pairs(order, place, own, phase, coher, slots, mine, band, staged, sems)
    for turn in range(GROUP - 1):
        member = lax.rem(place[1] + 1 + turn, GROUP)
        pairs.one(near.at[member], turn + 1, turn, sums[turn % len(sums)], first)
    pairs.finish(GROUP - 1)


def last_kernel(order, place, own, nine, ten, first, _p, _c, phase, coher, slots, mine, band, staged, sems, *sums):
    pairs = Pairs(order, place, own, phase, coher, slots, mine, band, staged, sems)
    pairs.one(nine, GROUP + 1, 0, sums[0], first)
    pairs.one(ten, GROUP + 2, 1, sums[1], first)
    pairs.finish(2)


def shifted(shard, by):
    length = lax.axis_size("date")
    return lax.ppermute(shard, "date", [(i, i - by) for i in range(by, length)])


def shards(slc, valid_rows, pair_order):
    _, _, height, width = slc.shape
    band = pair_order.shape[1]
    blocks = width // BLOCK
    cells = 2 * blocks
    rows = height + HALO
    core = lax.axis_index("row")
    rank = lax.rem(lax.axis_index("date"), GROUP)
    length = lax.axis_size("date")
    slab = slc[:, 0] * valid_rows.astype(jnp.bfloat16)[0][None, :, None]
    slab = slab.reshape(2, height, blocks, BLOCK).transpose(1, 0, 2, 3).reshape(height, cells, BLOCK)
    slab = jnp.where(core == 0, slab, slab[::-1])
    halo = lax.ppermute(slab[height - HALO :][::-1], "row", [(0, 1), (1, 0)])
    own = jnp.concatenate([slab, halo], axis=0)
    eight = shifted(own, GROUP)
    members = jnp.arange(GROUP)[:, None, None, None]
    given = jnp.where(members < rank, own[None], eight[None])
    groups = [list(range(g, g + GROUP)) for g in range(0, length, GROUP)]
    near = lax.all_to_all(given, "date", 0, 0, axis_index_groups=groups, tiled=True)
    nine = shifted(eight, 1)
    ten = shifted(eight, 2)
    place = jnp.stack([core, rank]).astype(jnp.int32)

    outs = (
        jax.ShapeDtypeStruct((2, band, height, width), jnp.bfloat16),
        jax.ShapeDtypeStruct((band, height, width), jnp.bfloat16),
    )
    kept = jax.ShapeDtypeStruct((blocks, height, BLOCK), jnp.float32)

    def scratch(turns, buffers):
        return [
            pltpu.SMEM((band,), jnp.int32),
            pltpu.VMEM((rows, cells, BLOCK), jnp.float32),
            pltpu.VMEM((3 * BLOCK, 2 * BLOCK), jnp.bfloat16),
            pltpu.VMEM((turns, 3, height, width), jnp.bfloat16),
            pltpu.SemaphoreType.DMA((turns, 2)),
        ] + [pltpu.VMEM((3, blocks * height, BLOCK), jnp.float32) for _ in range(buffers)]

    def cost(count):
        return pl.CostEstimate(flops=count << 23, bytes_accessed=count << 18, transcendentals=count << 15)

    params = pltpu.CompilerParams(vmem_limit_bytes=16 << 20)
    phase, coher, first = pl.pallas_call(
        first_kernel,
        out_shape=outs + (kept,),
        in_specs=[SCALARS, SCALARS, WHOLE, WHOLE],
        out_specs=(AWAY, AWAY, WHOLE),
        scratch_shapes=scratch(1, 2),
        compiler_params=params,
        cost_estimate=cost(1),
    )(pair_order, place, own, eight)
    phase, coher = pl.pallas_call(
        near_kernel,
        out_shape=outs,
        in_specs=[SCALARS, SCALARS, WHOLE, WHOLE, WHOLE, AWAY, AWAY],
        out_specs=(AWAY, AWAY),
        scratch_shapes=scratch(GROUP - 1, 2),
        input_output_aliases={5: 0, 6: 1},
        compiler_params=params,
        cost_estimate=cost(GROUP - 1),
    )(pair_order, place, own, near, first, phase, coher)
    phase, coher = pl.pallas_call(
        last_kernel,
        out_shape=outs,
        in_specs=[SCALARS, SCALARS, WHOLE, WHOLE, WHOLE, WHOLE, AWAY, AWAY],
        out_specs=(AWAY, AWAY),
        scratch_shapes=scratch(2, 2),
        input_output_aliases={6: 0, 7: 1},
        compiler_params=params,
        cost_estimate=cost(2),
    )(pair_order, place, own, nine, ten, first, phase, coher)
    return phase[:, None], coher[None]


def solution(mesh):
    placed = (P(None, "date", "row", None), P("date", "row"), P("date", None))
    return jax.shard_map(
        shards,
        mesh=mesh,
        in_specs=placed,
        out_specs=(P(None, "date", None, "row", None), P("date", None, "row", None)),
        check_vma=False,
    )
```

time: 138 us -> 40.4 us (0.29)
  waiting for transfers between devices: 66.1 us -> 11.6 us
  other arithmetic: 31.6 us -> 1.15 us
  starting transfers between devices: 31.2 us -> 18.9 us
  Pallas kernels: 0 us -> 6.2 us
  local copies, waits for them, and re-layouts: 7.4 us -> 1.44 us
    ppermute x12 -> x4, waiting for transfers between devices: 66.1 us -> 11.1 us  [the longest x3 9.97 us: shifted(): return lax.ppermute(shard, 'date', [(i, i - by) for i in range(by, length)])]
    add x7 -> x0, other arithmetic: 19.9 us -> none  [the longest x3 14.8 us: column_sum(): total = total + padded[..., offset:offset + width]]
    ppermute x12 -> x4, starting transfers between devices: 31.2 us -> 11.8 us  [the longest x3 9.87 us: shifted(): return lax.ppermute(shard, 'date', [(i, i - by) for i in range(by, length)])]
    all_to_all x0 -> x1, starting transfers between devices: none -> 7.1 us  [shards(): lax.all_to_all(given, 'date', 0, 0, axis_index_groups=groups, tiled=True)]
    pallas_call x0 -> x3, Pallas kernels: none -> 6.2 us  [the longest x1 2.8 us: shards(): pl.pallas_call(near_kernel, out_shape=outs, in_specs=[SCALARS, SCALARS, W...]
    gather x2 -> x0, local copies, waits for them, and re-layouts: 4.18 us -> none  [the longest x1 3.59 us: shards(): other = jnp.take(joined, local_idx, axis=1).astype(jnp.float32)]
    another operation x3 -> x1, other arithmetic: 3.93 us -> 0.08 us  [shards(): place = jnp.stack([core, rank]).astype(jnp.int32)]
    convert_element_type x3 -> x0, other arithmetic: 3.23 us -> none  [the longest x1 1.47 us: shards(): return (phase, coher.astype(jnp.bfloat16))]
  transfers between devices with their start and end apart: 12 -> 5, of which waited for: 7 -> 5; matrix products, arithmetic and copies ran while one was open for 2% -> 0% of each run, Pallas kernels for 0% -> 11%
where the time goes in v2:
time: 40.4 us; the launch traced here: 40 us
  starting transfers between devices  18.9 us (47%)
  waiting for transfers between devices  11.6 us (29%)
  Pallas kernels  6.2 us (15%)
  local copies, waits for them, and re-layouts  1.44 us (4%)
  other arithmetic  1.15 us (3%)
  between operations  0.77 us (2%)
    ppermute x3, waiting for transfers between devices, shifted(): return lax.ppermute(shard, 'date', [(i, i - by) for i in range(by, length)])  9.97 us
    ppermute x3, starting transfers between devices, shifted(): return lax.ppermute(shard, 'date', [(i, i - by) for i in range(by, length)])  9.87 us
    all_to_all x1, starting transfers between devices, shards(): lax.all_to_all(given, 'date', 0, 0, axis_index_groups=groups, tiled=True)  7.1 us
    pallas_call x1, Pallas kernels, shards(): pl.pallas_call(near_kernel, out_shape=outs, in_specs=[SCALARS, SCALARS, W...  2.8 us
    ppermute x1, starting transfers between devices, shards(): halo = lax.ppermute(slab[height - HALO:][::-1], 'row', [(0, 1), (1, 0)])  1.92 us
    pallas_call x1, Pallas kernels, shards(): pl.pallas_call(last_kernel, out_shape=outs, in_specs=[SCALARS, SCALARS, W...  1.8 us
    pallas_call x1, Pallas kernels, shards(): pl.pallas_call(first_kernel, out_shape=outs + (kept,), in_specs=[SCALARS,...  1.6 us
    unnamed x5, local copies, waits for them, and re-layouts  1.43 us
  transfers between devices with their start and end apart: 5, of which 5 were waited for; matrix products, arithmetic and copies ran while one was open for 0% of the time, Pallas kernels for 11%

profile of v2, /device:TPU:254, one launch (start us, length us, event | category | flops | bytes accessed | tf_op | source)
XLA Modules:
  0.0 40.0 jit_solution(13747897960341035104)
XLA Ops:
  0.6 0.0 copy-start.1
  0.6 0.9 %copy.11 = bf16[4,8,8,128]{3,2,1,0:T(8,128)(2,1)S(1)} copy(bf16[4,8,8,128]{3,1,2,0:T(8,128)(2,1)} %bitcast.24) | data formatting | bytes 131072
  1.5 0.0 copy-done.1
  1.5 0.1 fusion
  1.7 1.9 %collective-permute-start = (bf16[3,16,128]{2,1,0:T(8,128)(2,1)S(1)}, bf16[3,16,128]{2,1,0:T(8,128)(2,1)S(1)}, u32[]{:S(2)}, u32[]{:S(2)}) collective-permute-start(bf16[3,16,128]{2,1,0:T(8,128)(2,1)S(1)} %rev.7), channel_id=1, source_target_pairs={{0,1},{1,0},{2,3},{3,2},{4,5},{5,4},{6,7},{7,6},{8,9},{9,8},{10,11... | collective-permute-start | bytes 36872 | tf_op jit(solution)/shard_map/ppermute | solution.py:174
  3.6 1.1 %collective-permute-done = bf16[3,16,128]{2,1,0:T(8,128)(2,1)S(1)} collective-permute-done((bf16[3,16,128]{2,1,0:T(8,128)(2,1)S(1)}, bf16[3,16,128]{2,1,0:T(8,128)(2,1)S(1)}, u32[]{:S(2)}, u32[]{:S(2)}) %collective-permute-start) | collective-permute-done | bytes 12320 | tf_op jit(solution)/shard_map/ppermute | solution.py:174
  4.8 4.0 %collective-permute-start.1 = (bf16[19,16,128]{2,1,0:T(8,128)(2,1)S(1)}, bf16[19,16,128]{2,1,0:T(8,128)(2,1)S(1)}, u32[]{:S(2)}, u32[]{:S(2)}) collective-permute-start(bf16[19,16,128]{2,1,0:T(8,128)(2,1)S(1)} %pad_maximum_fusion.own), channel_id=1, source_target_pairs={{16,0},{18,2},{20,4},{22,6},{24,8},{26,10},{28,12},{30,14},{32,16}... | collective-permute-start | bytes 233480 | tf_op jit(solution)/shard_map/ppermute | solution.py:159
  8.8 6.6 %collective-permute-done.1.eight = bf16[19,16,128]{2,1,0:T(8,128)(2,1)S(1)} collective-permute-done((bf16[19,16,128]{2,1,0:T(8,128)(2,1)S(1)}, bf16[19,16,128]{2,1,0:T(8,128)(2,1)S(1)}, u32[]{:S(2)}, u32[]{:S(2)}) %collective-permute-start.1) | collective-permute-done | bytes 77856 | tf_op jit(solution)/shard_map/ppermute | solution.py:159
  15.4 0.9 %broadcast_select_fusion = bf16[8,19,16,128]{3,2,1,0:T(8,128)(2,1)} fusion(pred[8]{0:T(512)(128)(4,1)S(1)} %iota_compare_fusion, bf16[19,16,128]{2,1,0:T(8,128)(2,1)S(1)} %collective-permute-done.1.eight, bf16[19,16,128]{2,1,0:T(8,128)(2,1)S(1)} %pad_maximum_fusion.own), kind=kLoop, calls=%fused_computation | loop fusion | flops 311296 | bytes 778248 | tf_op jit(solution)/shard_map/jit(_where)/select_n | solution.py:178
  16.4 7.1 %all-to-all-start = ((bf16[8,19,16,128]{3,2,1,0:T(8,128)(2,1)}), bf16[8,19,16,128]{3,2,1,0:T(8,128)(2,1)S(1)}, u32[]{:S(2)}, u32[]{:S(2)}) async-start(bf16[8,19,16,128]{3,2,1,0:T(8,128)(2,1)} %broadcast_select_fusion), calls=%async_computation | async-start | bytes 1245184 | tf_op jit(solution)/shard_map/all_to_all | solution.py:180
  23.5 2.8 %collective-permute-start.2 = (bf16[19,16,128]{2,1,0:T(8,128)(2,1)S(1)}, bf16[19,16,128]{2,1,0:T(8,128)(2,1)S(1)}, u32[]{:S(2)}, u32[]{:S(2)}) collective-permute-start(bf16[19,16,128]{2,1,0:T(8,128)(2,1)S(1)} %collective-permute-done.1.eight), channel_id=1, source_target_pairs={{2,0},{4,2},{6,4},{8,6},{10,8},{12,10},{14,12},{16,14},{18,16},{20... | collective-permute-start | bytes 233480 | tf_op jit(solution)/shard_map/ppermute | solution.py:159
  26.2 3.1 %collective-permute-start.3 = (bf16[19,16,128]{2,1,0:T(8,128)(2,1)S(1)}, bf16[19,16,128]{2,1,0:T(8,128)(2,1)S(1)}, u32[]{:S(2)}, u32[]{:S(2)}) collective-permute-start(bf16[19,16,128]{2,1,0:T(8,128)(2,1)S(1)} %collective-permute-done.1.eight), channel_id=1, source_target_pairs={{4,0},{6,2},{8,4},{10,6},{12,8},{14,10},{16,12},{18,14},{20,16},{2... | collective-permute-start | bytes 233480 | tf_op jit(solution)/shard_map/ppermute | solution.py:159
  29.3 0.0 copy-start
  29.3 0.1 pad_add_fusion.place
  29.4 0.6 %copy-done = s32[1,10]{1,0:T(1,128)S(1)} copy-done((s32[1,10]{1,0:T(1,128)S(1)}, s32[1,10]{1,0:T(1,128)}, u32[]{:S(2)}) %copy-start) | copy-done | bytes 64
  30.0 1.6 %shard_map.50 = (bf16[2,10,16,1024]{3,2,1,0:T(8,128)(2,1)}, bf16[10,16,1024]{2,1,0:T(8,128)(2,1)}, f32[8,16,128]{2,1,0:T(8,128)S(1)}) custom-call(s32[1,10]{1,0:T(1,128)S(1)} %copy-done, s32[2]{0:T(128)S(1)} %pad_add_fusion.place, bf16[19,16,128]{2,1,0:T(8,128)(2,1)S(1)} %pad_maximum_fusion.own, bf16[19,16,128]{2,1,0:T(8,128)(2,1)S(1)} %collective-permute-done.1.eight), custom_call_target="tpu_custom_call" | custom-call | flops 8388608 | bytes 262144 | tf_op jit(solution)/shard_map/pallas_call | solution.py:204
  31.6 0.5 %all-to-all-done.near = bf16[8,19,16,128]{3,2,1,0:T(8,128)(2,1)S(1)} async-done(((bf16[8,19,16,128]{3,2,1,0:T(8,128)(2,1)}), bf16[8,19,16,128]{3,2,1,0:T(8,128)(2,1)S(1)}, u32[]{:S(2)}, u32[]{:S(2)}) %all-to-all-start) | async-done | bytes 622624 | tf_op jit(solution)/shard_map/all_to_all | solution.py:180
  32.1 2.8 %shard_map.51 = (bf16[2,10,16,1024]{3,2,1,0:T(8,128)(2,1)}, bf16[10,16,1024]{2,1,0:T(8,128)(2,1)}) custom-call(s32[1,10]{1,0:T(1,128)S(1)} %copy-done, s32[2]{0:T(128)S(1)} %pad_add_fusion.place, bf16[19,16,128]{2,1,0:T(8,128)(2,1)S(1)} %pad_maximum_fusion.own, ...), custom_call_target="tpu_custom_call", output_to_operand_aliasing={{0}: (5, {}), {1}: (6, {})} | custom-call | flops 58720256 | bytes 1835008 | tf_op jit(solution)/shard_map/pallas_call | solution.py:213
  34.9 0.3 collective-permute-done.2.nine
  35.2 3.1 %collective-permute-done.3.ten = bf16[19,16,128]{2,1,0:T(8,128)(2,1)S(1)} collective-permute-done((bf16[19,16,128]{2,1,0:T(8,128)(2,1)S(1)}, bf16[19,16,128]{2,1,0:T(8,128)(2,1)S(1)}, u32[]{:S(2)}, u32[]{:S(2)}) %collective-permute-start.3) | collective-permute-done | bytes 77856 | tf_op jit(solution)/shard_map/ppermute | solution.py:159
  38.2 1.8 %shard_map.52 = (bf16[2,10,16,1024]{3,2,1,0:T(8,128)(2,1)}, bf16[10,16,1024]{2,1,0:T(8,128)(2,1)}) custom-call(s32[1,10]{1,0:T(1,128)S(1)} %copy-done, s32[2]{0:T(128)S(1)} %pad_add_fusion.place, bf16[19,16,128]{2,1,0:T(8,128)(2,1)S(1)} %pad_maximum_fusion.own, ...), custom_call_target="tpu_custom_call", output_to_operand_aliasing={{0}: (6, {}), {1}: (7, {})} | custom-call | flops 16777216 | bytes 524288 | tf_op jit(solution)/shard_map/pallas_call | solution.py:223
  (6 shorter events, 0.1 us)
Async XLA Ops:
  0.6 0.9 %copy-start.1 = (s32[1,16]{1,0:T(1,128)S(1)}, s32[1,16]{1,0:T(1,128)}, u32[]{:S(2)}) copy-start(s32[1,16]{1,0:T(1,128)} %param.4) | copy-start | bytes 196
  1.7 3.1 %collective-permute-start = (bf16[3,16,128]{2,1,0:T(8,128)(2,1)S(1)}, bf16[3,16,128]{2,1,0:T(8,128)(2,1)S(1)}, u32[]{:S(2)}, u32[]{:S(2)}) collective-permute-start(bf16[3,16,128]{2,1,0:T(8,128)(2,1)S(1)} %rev.7), channel_id=1, source_target_pairs={{0,1},{1,0},{2,3},{3,2},{4,5},{5,4},{6,7},{7,6},{8,9},{9,8},{10,11... | collective-permute-start | bytes 36872 | tf_op jit(solution)/shard_map/ppermute | solution.py:174
  4.8 10.7 %collective-permute-start.1 = (bf16[19,16,128]{2,1,0:T(8,128)(2,1)S(1)}, bf16[19,16,128]{2,1,0:T(8,128)(2,1)S(1)}, u32[]{:S(2)}, u32[]{:S(2)}) collective-permute-start(bf16[19,16,128]{2,1,0:T(8,128)(2,1)S(1)} %pad_maximum_fusion.own), channel_id=1, source_target_pairs={{16,0},{18,2},{20,4},{22,6},{24,8},{26,10},{28,12},{30,14},{32,16}... | collective-permute-start | bytes 233480 | tf_op jit(solution)/shard_map/ppermute | solution.py:159
  16.4 15.7 %all-to-all-start = ((bf16[8,19,16,128]{3,2,1,0:T(8,128)(2,1)}), bf16[8,19,16,128]{3,2,1,0:T(8,128)(2,1)S(1)}, u32[]{:S(2)}, u32[]{:S(2)}) async-start(bf16[8,19,16,128]{3,2,1,0:T(8,128)(2,1)} %broadcast_select_fusion), calls=%async_computation | async-start | bytes 1245184 | tf_op jit(solution)/shard_map/all_to_all | solution.py:180
  23.5 11.7 %collective-permute-start.2 = (bf16[19,16,128]{2,1,0:T(8,128)(2,1)S(1)}, bf16[19,16,128]{2,1,0:T(8,128)(2,1)S(1)}, u32[]{:S(2)}, u32[]{:S(2)}) collective-permute-start(bf16[19,16,128]{2,1,0:T(8,128)(2,1)S(1)} %collective-permute-done.1.eight), channel_id=1, source_target_pairs={{2,0},{4,2},{6,4},{8,6},{10,8},{12,10},{14,12},{16,14},{18,16},{20... | collective-permute-start | bytes 233480 | tf_op jit(solution)/shard_map/ppermute | solution.py:159
  26.2 12.0 %collective-permute-start.3 = (bf16[19,16,128]{2,1,0:T(8,128)(2,1)S(1)}, bf16[19,16,128]{2,1,0:T(8,128)(2,1)S(1)}, u32[]{:S(2)}, u32[]{:S(2)}) collective-permute-start(bf16[19,16,128]{2,1,0:T(8,128)(2,1)S(1)} %collective-permute-done.1.eight), channel_id=1, source_target_pairs={{4,0},{6,2},{8,4},{10,6},{12,8},{14,10},{16,12},{18,14},{20,16},{2... | collective-permute-start | bytes 233480 | tf_op jit(solution)/shard_map/ppermute | solution.py:159
  29.3 0.7 %copy-start = (s32[1,10]{1,0:T(1,128)S(1)}, s32[1,10]{1,0:T(1,128)}, u32[]{:S(2)}) copy-start(s32[1,10]{1,0:T(1,128)} %order.5) | copy-start | bytes 124

commit v3 on v2

--- a/solution.py
+++ b/solution.py
@@ -6,6 +6,7 @@
 from jax.sharding import PartitionSpec as P
 
 GROUP = 8
+PLANE = 32
 HALO = 3
 BLOCK = 128
 TINY = 1.1754944e-38
@@ -108,7 +109,7 @@
         columns = [Column() for _ in range(3)]
         for row in range(self.rows):
             a0, a1 = self.mine[row, : self.cells], self.mine[row, self.cells :]
-            b = other[row].astype(jnp.float32)
+            b = other(row)
             b0, b1 = b[: self.cells], b[self.cells :]
             values = (a0 * b0 + a1 * b1, a1 * b0 - a0 * b1, b0 * b0 + b1 * b1)
             for index, value in enumerate(values):
@@ -132,10 +133,10 @@
                 copy.wait()
 
 
-def first_kernel(order, place, own, eight, phase, coher, first, slots, mine, band, staged, sems, *sums):
+def first_kernel(order, place, own, eight, _n, _t, phase, coher, first, slots, mine, band, staged, sems, *sums):
     pairs = Pairs(order, place, own, phase, coher, slots, mine, band, staged, sems)
     pairs.own_intensity(sums[1], first)
-    pairs.one(eight, GROUP, 0, sums[0], first)
+    pairs.one(lambda row: eight[row].astype(jnp.float32), GROUP, 0, sums[0], first)
     pairs.finish(1)
 
 
@@ -143,20 +144,22 @@
     pairs = Pairs(order, place, own, phase, coher, slots, mine, band, staged, sems)
     for turn in range(GROUP - 1):
         member = lax.rem(place[1] + 1 + turn, GROUP)
-        pairs.one(near.at[member], turn + 1, turn, sums[turn % len(sums)], first)
+        pairs.one(lambda row: near[member, row].astype(jnp.float32), turn + 1, turn, sums[turn % len(sums)], first)
     pairs.finish(GROUP - 1)
 
 
-def last_kernel(order, place, own, nine, ten, first, _p, _c, phase, coher, slots, mine, band, staged, sems, *sums):
+def last_kernel(order, place, own, nine, nine_far, ten, ten_far, first, _p, _c, phase, coher, slots, mine, band, staged, sems, *sums):
     pairs = Pairs(order, place, own, phase, coher, slots, mine, band, staged, sems)
-    pairs.one(nine, GROUP + 1, 0, sums[0], first)
-    pairs.one(ten, GROUP + 2, 1, sums[1], first)
+    for turn, (by_group, far) in enumerate(((nine, nine_far), (ten, ten_far)), 0):
+        pairs.one(
+            lambda row: by_group[row].astype(jnp.float32) + far[row].astype(jnp.float32),
+            GROUP + 1 + turn, turn, sums[turn % len(sums)], first,
+        )
     pairs.finish(2)
 
 
-def shifted(shard, by):
-    length = lax.axis_size("date")
-    return lax.ppermute(shard, "date", [(i, i - by) for i in range(by, length)])
+def moved(shard, pairs):
+    return lax.ppermute(shard, "date", pairs)
 
 
 def shards(slc, valid_rows, pair_order):
@@ -173,13 +176,17 @@
     slab = jnp.where(core == 0, slab, slab[::-1])
     halo = lax.ppermute(slab[height - HALO :][::-1], "row", [(0, 1), (1, 0)])
     own = jnp.concatenate([slab, halo], axis=0)
-    eight = shifted(own, GROUP)
+    eight = moved(own, [(i, i - GROUP) for i in range(GROUP, length)])
+    ends = range(PLANE, length, PLANE)
+    nine_far = moved(own, [(z + GROUP, z - 1) for z in ends])
+    ten_far = moved(own, [(z + GROUP + i, z - 2 + i) for z in ends for i in range(2)])
     members = jnp.arange(GROUP)[:, None, None, None]
     given = jnp.where(members < rank, own[None], eight[None])
     groups = [list(range(g, g + GROUP)) for g in range(0, length, GROUP)]
     near = lax.all_to_all(given, "date", 0, 0, axis_index_groups=groups, tiled=True)
-    nine = shifted(eight, 1)
-    ten = shifted(eight, 2)
+    nine, ten = (
+        moved(eight, [(i, i - by) for i in range(length) if i % PLANE >= by]) for by in (1, 2)
+    )
     place = jnp.stack([core, rank]).astype(jnp.int32)
 
     outs = (
@@ -198,18 +205,18 @@
         ] + [pltpu.VMEM((3, blocks * height, BLOCK), jnp.float32) for _ in range(buffers)]
 
     def cost(count):
-        return pl.CostEstimate(flops=count << 23, bytes_accessed=count << 18, transcendentals=count << 15)
+        return pl.CostEstimate(flops=count << 33, bytes_accessed=count << 23, transcendentals=count << 15)
 
     params = pltpu.CompilerParams(vmem_limit_bytes=16 << 20)
     phase, coher, first = pl.pallas_call(
         first_kernel,
         out_shape=outs + (kept,),
-        in_specs=[SCALARS, SCALARS, WHOLE, WHOLE],
+        in_specs=[SCALARS, SCALARS, WHOLE, WHOLE, AWAY, AWAY],
         out_specs=(AWAY, AWAY, WHOLE),
         scratch_shapes=scratch(1, 2),
         compiler_params=params,
-        cost_estimate=cost(1),
-    )(pair_order, place, own, eight)
+        cost_estimate=cost(3),
+    )(pair_order, place, own, eight, nine_far, ten_far)
     phase, coher = pl.pallas_call(
         near_kernel,
         out_shape=outs,
@@ -223,13 +230,13 @@
     phase, coher = pl.pallas_call(
         last_kernel,
         out_shape=outs,
-        in_specs=[SCALARS, SCALARS, WHOLE, WHOLE, WHOLE, WHOLE, AWAY, AWAY],
+        in_specs=[SCALARS, SCALARS] + [WHOLE] * 6 + [AWAY, AWAY],
         out_specs=(AWAY, AWAY),
         scratch_shapes=scratch(2, 2),
-        input_output_aliases={6: 0, 7: 1},
+        input_output_aliases={8: 0, 9: 1},
         compiler_params=params,
         cost_estimate=cost(2),
-    )(pair_order, place, own, nine, ten, first, phase, coher)
+    )(pair_order, place, own, nine, nine_far, ten, ten_far, first, phase, coher)
     return phase[:, None], coher[None]
 
 

time: 40.4 us -> 38.5 us (0.953)
  the two profiles are of different devices: /device:TPU:254 before, /device:TPU:251 now
where the time goes in v3:
time: 38.5 us; the launch traced here: 38.2 us
  starting transfers between devices  21.2 us (55%)
  waiting for transfers between devices  7.94 us (21%)
  Pallas kernels  6.22 us (16%)
  other arithmetic  1.15 us (3%)
  local copies, waits for them, and re-layouts  0.87 us (2%)
  between operations  0.81 us (2%)
    ppermute x5, starting transfers between devices, moved(): return lax.ppermute(shard, 'date', pairs)  11.2 us
    all_to_all x1, starting transfers between devices, shards(): lax.all_to_all(given, 'date', 0, 0, axis_index_groups=groups, tiled=True)  7.34 us
    ppermute x5, waiting for transfers between devices, moved(): return lax.ppermute(shard, 'date', pairs)  5.11 us
    pallas_call x1, Pallas kernels, shards(): pl.pallas_call(near_kernel, out_shape=outs, in_specs=[SCALARS, SCALARS, W...  2.79 us
    ppermute x1, starting transfers between devices, shards(): halo = lax.ppermute(slab[height - HALO:][::-1], 'row', [(0, 1), (1, 0)])  2.58 us
    all_to_all x1, waiting for transfers between devices, shards(): lax.all_to_all(given, 'date', 0, 0, axis_index_groups=groups, tiled=True)  2.03 us
    pallas_call x1, Pallas kernels, shards(): pl.pallas_call(last_kernel, out_shape=outs, in_specs=[SCALARS, SCALARS] +...  1.82 us
    pallas_call x1, Pallas kernels, shards(): pl.pallas_call(first_kernel, out_shape=outs + (kept,), in_specs=[SCALARS,...  1.61 us
  transfers between devices with their start and end apart: 7, of which 4 were waited for; matrix products, arithmetic and copies ran while one was open for 3% of the time, Pallas kernels for 12%

profile of v3, /device:TPU:251, one launch (start us, length us, event | category | flops | bytes accessed | tf_op | source)
XLA Modules:
  0.0 38.2 jit_solution(14140052326730252538)
XLA Ops:
  0.6 0.0 copy-start.1
  0.6 0.9 %copy.11 = bf16[4,8,8,128]{3,2,1,0:T(8,128)(2,1)S(1)} copy(bf16[4,8,8,128]{3,1,2,0:T(8,128)(2,1)} %bitcast.22) | data formatting | bytes 131072
  1.5 0.0 copy-done.1
  1.5 0.1 fusion
  1.7 2.6 %collective-permute-start = (bf16[3,16,128]{2,1,0:T(8,128)(2,1)S(1)}, bf16[3,16,128]{2,1,0:T(8,128)(2,1)S(1)}, u32[]{:S(2)}, u32[]{:S(2)}) collective-permute-start(bf16[3,16,128]{2,1,0:T(8,128)(2,1)S(1)} %rev.7), channel_id=1, source_target_pairs={{0,1},{1,0},{2,3},{3,2},{4,5},{5,4},{6,7},{7,6},{8,9},{9,8},{10,11... | collective-permute-start | bytes 36872 | tf_op jit(solution)/shard_map/ppermute | solution.py:177
  4.3 0.8 %collective-permute-done = bf16[3,16,128]{2,1,0:T(8,128)(2,1)S(1)} collective-permute-done((bf16[3,16,128]{2,1,0:T(8,128)(2,1)S(1)}, bf16[3,16,128]{2,1,0:T(8,128)(2,1)S(1)}, u32[]{:S(2)}, u32[]{:S(2)}) %collective-permute-start) | collective-permute-done | bytes 12320 | tf_op jit(solution)/shard_map/ppermute | solution.py:177
  5.1 3.8 %collective-permute-start.1 = (bf16[19,16,128]{2,1,0:T(8,128)(2,1)S(1)}, bf16[19,16,128]{2,1,0:T(8,128)(2,1)S(1)}, u32[]{:S(2)}, u32[]{:S(2)}) collective-permute-start(bf16[19,16,128]{2,1,0:T(8,128)(2,1)S(1)} %pad_maximum_fusion.own), channel_id=1, source_target_pairs={{16,0},{18,2},{20,4},{22,6},{24,8},{26,10},{28,12},{30,14},{32,16}... | collective-permute-start | bytes 233480 | tf_op jit(solution)/shard_map/ppermute | solution.py:162
  8.9 0.1 pad_add_fusion.place
  8.9 0.7 %collective-permute-start.3 = (bf16[19,16,128]{2,1,0:T(8,128)(2,1)S(1)}, bf16[19,16,128]{2,1,0:T(8,128)(2,1)S(1)}, u32[]{:S(2)}, u32[]{:S(2)}) collective-permute-start(bf16[19,16,128]{2,1,0:T(8,128)(2,1)S(1)} %pad_maximum_fusion.own), channel_id=1, source_target_pairs={{80,62},{144,126},{208,190},{272,254},{336,318},{400,382},{464,446... | collective-permute-start | bytes 233480 | tf_op jit(solution)/shard_map/ppermute | solution.py:162
  9.6 0.7 %collective-permute-start.5 = (bf16[19,16,128]{2,1,0:T(8,128)(2,1)S(1)}, bf16[19,16,128]{2,1,0:T(8,128)(2,1)S(1)}, u32[]{:S(2)}, u32[]{:S(2)}) collective-permute-start(bf16[19,16,128]{2,1,0:T(8,128)(2,1)S(1)} %pad_maximum_fusion.own), channel_id=1, source_target_pairs={{80,60},{82,62},{144,124},{146,126},{208,188},{210,190},{272,252},... | collective-permute-start | bytes 233480 | tf_op jit(solution)/shard_map/ppermute | solution.py:162
  10.3 4.6 %collective-permute-done.1.eight = bf16[19,16,128]{2,1,0:T(8,128)(2,1)S(1)} collective-permute-done((bf16[19,16,128]{2,1,0:T(8,128)(2,1)S(1)}, bf16[19,16,128]{2,1,0:T(8,128)(2,1)S(1)}, u32[]{:S(2)}, u32[]{:S(2)}) %collective-permute-start.1) | collective-permute-done | bytes 77856 | tf_op jit(solution)/shard_map/ppermute | solution.py:162
  14.9 1.0 %broadcast_select_fusion = bf16[8,19,16,128]{3,2,1,0:T(8,128)(2,1)} fusion(pred[8]{0:T(512)(128)(4,1)S(1)} %iota_compare_fusion, bf16[19,16,128]{2,1,0:T(8,128)(2,1)S(1)} %collective-permute-done.1.eight, bf16[19,16,128]{2,1,0:T(8,128)(2,1)S(1)} %pad_maximum_fusion.own), kind=kLoop, calls=%fused_computation | loop fusion | flops 311296 | bytes 778248 | tf_op jit(solution)/shard_map/jit(_where)/select_n | solution.py:184
  15.8 0.0 copy-start
  15.8 7.3 %all-to-all-start = ((bf16[8,19,16,128]{3,2,1,0:T(8,128)(2,1)}), bf16[8,19,16,128]{3,2,1,0:T(8,128)(2,1)S(1)}, u32[]{:S(2)}, u32[]{:S(2)}) async-start(bf16[8,19,16,128]{3,2,1,0:T(8,128)(2,1)} %broadcast_select_fusion), calls=%async_computation | async-start | bytes 1245184 | tf_op jit(solution)/shard_map/all_to_all | solution.py:186
  23.1 2.2 %collective-permute-start.2 = (bf16[19,16,128]{2,1,0:T(8,128)(2,1)S(1)}, bf16[19,16,128]{2,1,0:T(8,128)(2,1)S(1)}, u32[]{:S(2)}, u32[]{:S(2)}) collective-permute-start(bf16[19,16,128]{2,1,0:T(8,128)(2,1)S(1)} %collective-permute-done.1.eight), channel_id=1, source_target_pairs={{2,0},{4,2},{6,4},{8,6},{10,8},{12,10},{14,12},{16,14},{18,16},{20... | collective-permute-start | bytes 233480 | tf_op jit(solution)/shard_map/ppermute | solution.py:162
  25.3 4.0 %collective-permute-start.4 = (bf16[19,16,128]{2,1,0:T(8,128)(2,1)S(1)}, bf16[19,16,128]{2,1,0:T(8,128)(2,1)S(1)}, u32[]{:S(2)}, u32[]{:S(2)}) collective-permute-start(bf16[19,16,128]{2,1,0:T(8,128)(2,1)S(1)} %collective-permute-done.1.eight), channel_id=1, source_target_pairs={{4,0},{6,2},{8,4},{10,6},{12,8},{14,10},{16,12},{18,14},{20,16},{2... | collective-permute-start | bytes 233480 | tf_op jit(solution)/shard_map/ppermute | solution.py:162
  29.3 0.0 collective-permute-done.3._n.nine_far
  29.3 0.0 collective-permute-done.5._t.ten_far
  29.4 0.0 copy-done
  29.4 1.6 %shard_map.50 = (bf16[2,10,16,1024]{3,2,1,0:T(8,128)(2,1)}, bf16[10,16,1024]{2,1,0:T(8,128)(2,1)}, f32[8,16,128]{2,1,0:T(8,128)S(1)}) custom-call(s32[1,10]{1,0:T(1,128)S(1)} %copy-done, s32[2]{0:T(128)S(1)} %pad_add_fusion.place, bf16[19,16,128]{2,1,0:T(8,128)(2,1)S(1)} %pad_maximum_fusion.own, bf16[19,16,128]{2,1,0:T(8,128)(2,1)S(1)} %collective-permute-done.1.eight, ...), custom_call_target="tpu_custom_call" | custom-call | flops 25769803776 | bytes 25165824 | tf_op jit(solution)/shard_map/pallas_call | solution.py:211
  31.0 2.0 %all-to-all-done.near = bf16[8,19,16,128]{3,2,1,0:T(8,128)(2,1)S(1)} async-done(((bf16[8,19,16,128]{3,2,1,0:T(8,128)(2,1)}), bf16[8,19,16,128]{3,2,1,0:T(8,128)(2,1)S(1)}, u32[]{:S(2)}, u32[]{:S(2)}) %all-to-all-start) | async-done | bytes 622624 | tf_op jit(solution)/shard_map/all_to_all | solution.py:186
  33.0 2.8 %shard_map.51 = (bf16[2,10,16,1024]{3,2,1,0:T(8,128)(2,1)}, bf16[10,16,1024]{2,1,0:T(8,128)(2,1)}) custom-call(s32[1,10]{1,0:T(1,128)S(1)} %copy-done, s32[2]{0:T(128)S(1)} %pad_add_fusion.place, bf16[19,16,128]{2,1,0:T(8,128)(2,1)S(1)} %pad_maximum_fusion.own, ...), custom_call_target="tpu_custom_call", output_to_operand_aliasing={{0}: (5, {}), {1}: (6, {})} | custom-call | flops 60129542144 | bytes 58720256 | tf_op jit(solution)/shard_map/pallas_call | solution.py:220
  35.8 0.0 collective-permute-done.2.nine
  35.8 0.5 %collective-permute-done.4.ten = bf16[19,16,128]{2,1,0:T(8,128)(2,1)S(1)} collective-permute-done((bf16[19,16,128]{2,1,0:T(8,128)(2,1)S(1)}, bf16[19,16,128]{2,1,0:T(8,128)(2,1)S(1)}, u32[]{:S(2)}, u32[]{:S(2)}) %collective-permute-start.4) | collective-permute-done | bytes 77856 | tf_op jit(solution)/shard_map/ppermute | solution.py:162
  36.3 1.8 %shard_map.52 = (bf16[2,10,16,1024]{3,2,1,0:T(8,128)(2,1)}, bf16[10,16,1024]{2,1,0:T(8,128)(2,1)}) custom-call(s32[1,10]{1,0:T(1,128)S(1)} %copy-done, s32[2]{0:T(128)S(1)} %pad_add_fusion.place, bf16[19,16,128]{2,1,0:T(8,128)(2,1)S(1)} %pad_maximum_fusion.own, ...), custom_call_target="tpu_custom_call", output_to_operand_aliasing={{0}: (8, {}), {1}: (9, {})} | custom-call | flops 17179869184 | bytes 16777216 | tf_op jit(solution)/shard_map/pallas_call | solution.py:230
  (6 shorter events, 0.0 us)
Async XLA Ops:
  0.6 0.9 %copy-start.1 = (s32[1,16]{1,0:T(1,128)S(1)}, s32[1,16]{1,0:T(1,128)}, u32[]{:S(2)}) copy-start(s32[1,16]{1,0:T(1,128)} %param.4) | copy-start | bytes 196
  1.7 3.4 %collective-permute-start = (bf16[3,16,128]{2,1,0:T(8,128)(2,1)S(1)}, bf16[3,16,128]{2,1,0:T(8,128)(2,1)S(1)}, u32[]{:S(2)}, u32[]{:S(2)}) collective-permute-start(bf16[3,16,128]{2,1,0:T(8,128)(2,1)S(1)} %rev.7), channel_id=1, source_target_pairs={{0,1},{1,0},{2,3},{3,2},{4,5},{5,4},{6,7},{7,6},{8,9},{9,8},{10,11... | collective-permute-start | bytes 36872 | tf_op jit(solution)/shard_map/ppermute | solution.py:177
  5.1 9.8 %collective-permute-start.1 = (bf16[19,16,128]{2,1,0:T(8,128)(2,1)S(1)}, bf16[19,16,128]{2,1,0:T(8,128)(2,1)S(1)}, u32[]{:S(2)}, u32[]{:S(2)}) collective-permute-start(bf16[19,16,128]{2,1,0:T(8,128)(2,1)S(1)} %pad_maximum_fusion.own), channel_id=1, source_target_pairs={{16,0},{18,2},{20,4},{22,6},{24,8},{26,10},{28,12},{30,14},{32,16}... | collective-permute-start | bytes 233480 | tf_op jit(solution)/shard_map/ppermute | solution.py:162
  8.9 20.4 %collective-permute-start.3 = (bf16[19,16,128]{2,1,0:T(8,128)(2,1)S(1)}, bf16[19,16,128]{2,1,0:T(8,128)(2,1)S(1)}, u32[]{:S(2)}, u32[]{:S(2)}) collective-permute-start(bf16[19,16,128]{2,1,0:T(8,128)(2,1)S(1)} %pad_maximum_fusion.own), channel_id=1, source_target_pairs={{80,62},{144,126},{208,190},{272,254},{336,318},{400,382},{464,446... | collective-permute-start | bytes 233480 | tf_op jit(solution)/shard_map/ppermute | solution.py:162
  9.6 19.7 %collective-permute-start.5 = (bf16[19,16,128]{2,1,0:T(8,128)(2,1)S(1)}, bf16[19,16,128]{2,1,0:T(8,128)(2,1)S(1)}, u32[]{:S(2)}, u32[]{:S(2)}) collective-permute-start(bf16[19,16,128]{2,1,0:T(8,128)(2,1)S(1)} %pad_maximum_fusion.own), channel_id=1, source_target_pairs={{80,60},{82,62},{144,124},{146,126},{208,188},{210,190},{272,252},... | collective-permute-start | bytes 233480 | tf_op jit(solution)/shard_map/ppermute | solution.py:162
  15.8 13.5 %copy-start = (s32[1,10]{1,0:T(1,128)S(1)}, s32[1,10]{1,0:T(1,128)}, u32[]{:S(2)}) copy-start(s32[1,10]{1,0:T(1,128)} %order.5) | copy-start | bytes 124
  15.8 17.2 %all-to-all-start = ((bf16[8,19,16,128]{3,2,1,0:T(8,128)(2,1)}), bf16[8,19,16,128]{3,2,1,0:T(8,128)(2,1)S(1)}, u32[]{:S(2)}, u32[]{:S(2)}) async-start(bf16[8,19,16,128]{3,2,1,0:T(8,128)(2,1)} %broadcast_select_fusion), calls=%async_computation | async-start | bytes 1245184 | tf_op jit(solution)/shard_map/all_to_all | solution.py:186
  23.1 12.7 %collective-permute-start.2 = (bf16[19,16,128]{2,1,0:T(8,128)(2,1)S(1)}, bf16[19,16,128]{2,1,0:T(8,128)(2,1)S(1)}, u32[]{:S(2)}, u32[]{:S(2)}) collective-permute-start(bf16[19,16,128]{2,1,0:T(8,128)(2,1)S(1)} %collective-permute-done.1.eight), channel_id=1, source_target_pairs={{2,0},{4,2},{6,4},{8,6},{10,8},{12,10},{14,12},{16,14},{18,16},{20... | collective-permute-start | bytes 233480 | tf_op jit(solution)/shard_map/ppermute | solution.py:162
  25.3 11.0 %collective-permute-start.4 = (bf16[19,16,128]{2,1,0:T(8,128)(2,1)S(1)}, bf16[19,16,128]{2,1,0:T(8,128)(2,1)S(1)}, u32[]{:S(2)}, u32[]{:S(2)}) collective-permute-start(bf16[19,16,128]{2,1,0:T(8,128)(2,1)S(1)} %collective-permute-done.1.eight), channel_id=1, source_target_pairs={{4,0},{6,2},{8,4},{10,6},{12,8},{14,10},{16,12},{18,14},{20,16},{2... | collective-permute-start | bytes 233480 | tf_op jit(solution)/shard_map/ppermute | solution.py:162

commit v4 on v3

--- a/solution.py
+++ b/solution.py
@@ -7,6 +7,7 @@
 
 GROUP = 8
 PLANE = 32
+LEFT = 3
 HALO = 3
 BLOCK = 128
 TINY = 1.1754944e-38
@@ -68,17 +69,14 @@
 
 
 class Pairs:
-    def __init__(self, order, place, own, phase, coher, slots, mine, band, staged, sems):
+    def __init__(self, order, place, phase, coher, slots, mine, band, staged, sems):
         self.core = place[0]
         self.phase, self.coher = phase, coher
         self.slots, self.mine, self.band, self.staged, self.sems = slots, mine, band, staged, sems
-        self.rows, self.cells = own.shape[0], own.shape[1] // 2
-        self.height, self.blocks = self.rows - HALO, own.shape[1] // 2
+        self.rows, self.cells = mine.shape[0], mine.shape[1] // 2
+        self.height, self.blocks = self.rows - HALO, mine.shape[1] // 2
         for j in range(order.shape[1]):
             slots[order[0, j]] = j
-        for row in range(self.rows):
-            mine[row] = own[row].astype(jnp.float32)
-        band_matrix(band)
 
     def store(self, sums, index, row, value):
         if value is not None:
@@ -97,15 +95,18 @@
             self.store(sums, 0, row, column.feed(a0 * a0 + a1 * a1))
         first[...] = self.boxes(sums, 1)[0]
 
-    def copies(self, turn, slot):
-        kept, sems = self.staged.at[turn], self.sems.at[turn]
+    def copies(self, kept, sem, slot):
+        sems = self.sems.at[sem]
         return (
             pltpu.make_async_copy(kept.at[0:2], self.phase.at[:, slot], sems.at[0]),
             pltpu.make_async_copy(kept.at[2], self.coher.at[slot], sems.at[1]),
         )
 
-    def one(self, other, offset, turn, sums, first):
-        slot = self.slots[offset - 1]
+    def send(self, kept, sem, offset):
+        for copy in self.copies(kept, sem, self.slots[offset - 1]):
+            copy.start()
+
+    def one(self, other, kept, sums, first):
         columns = [Column() for _ in range(3)]
         for row in range(self.rows):
             a0, a1 = self.mine[row, : self.cells], self.mine[row, self.cells :]
@@ -123,39 +124,49 @@
         for index, value in enumerate((re * scale, im * scale, co)):
             value = value.astype(jnp.bfloat16)
             for b in range(self.blocks):
-                self.staged[turn, index, :, b * BLOCK : (b + 1) * BLOCK] = value[b]
-        for copy in self.copies(turn, slot):
-            copy.start()
-
-    def finish(self, turns):
-        for turn in range(turns):
-            for copy in self.copies(turn, 0):
+                kept[index, :, b * BLOCK : (b + 1) * BLOCK] = value[b]
+
+    def finish(self, kepts):
+        for sem, kept in enumerate(kepts):
+            for copy in self.copies(kept, sem, 0):
                 copy.wait()
 
 
-def first_kernel(order, place, own, eight, _n, _t, phase, coher, first, slots, mine, band, staged, sems, *sums):
-    pairs = Pairs(order, place, own, phase, coher, slots, mine, band, staged, sems)
+def first_kernel(order, place, own, eight, _n, _t, phase, coher, first, mine, band, slots, staged, sems, *sums):
+    for row in range(own.shape[0]):
+        mine[row] = own[row].astype(jnp.float32)
+    band_matrix(band)
+    pairs = Pairs(order, place, phase, coher, slots, mine, band, staged, sems)
     pairs.own_intensity(sums[1], first)
-    pairs.one(lambda row: eight[row].astype(jnp.float32), GROUP, 0, sums[0], first)
-    pairs.finish(1)
-
-
-def near_kernel(order, place, own, near, first, _p, _c, phase, coher, slots, mine, band, staged, sems, *sums):
-    pairs = Pairs(order, place, own, phase, coher, slots, mine, band, staged, sems)
+    pairs.one(lambda row: eight[row].astype(jnp.float32), staged.at[0], sums[0], first)
+    pairs.send(staged.at[0], 0, GROUP)
+    pairs.finish([staged.at[0]])
+
+
+def near_kernel(order, place, near, first, mine, band, _p, _c, phase, coher, left, slots, staged, sems, *sums):
+    pairs = Pairs(order, place, phase, coher, slots, mine, band, staged, sems)
+    sent = GROUP - 1 - LEFT
     for turn in range(GROUP - 1):
         member = lax.rem(place[1] + 1 + turn, GROUP)
-        pairs.one(lambda row: near[member, row].astype(jnp.float32), turn + 1, turn, sums[turn % len(sums)], first)
-    pairs.finish(GROUP - 1)
-
-
-def last_kernel(order, place, own, nine, nine_far, ten, ten_far, first, _p, _c, phase, coher, slots, mine, band, staged, sems, *sums):
-    pairs = Pairs(order, place, own, phase, coher, slots, mine, band, staged, sems)
-    for turn, (by_group, far) in enumerate(((nine, nine_far), (ten, ten_far)), 0):
+        kept = staged.at[turn] if turn < sent else left.at[turn - sent]
+        pairs.one(lambda row: near[member, row].astype(jnp.float32), kept, sums[turn % len(sums)], first)
+        if turn < sent:
+            pairs.send(kept, turn, turn + 1)
+    pairs.finish([staged.at[turn] for turn in range(sent)])
+
+
+def last_kernel(order, place, left, nine, nine_far, ten, ten_far, first, mine, band, _p, _c, phase, coher, slots, staged, sems, *sums):
+    pairs = Pairs(order, place, phase, coher, slots, mine, band, staged, sems)
+    kepts = [left.at[turn] for turn in range(LEFT)] + [staged.at[turn] for turn in range(2)]
+    for turn in range(LEFT):
+        pairs.send(kepts[turn], turn, GROUP - LEFT + turn)
+    for turn, (by_group, far) in enumerate(((nine, nine_far), (ten, ten_far))):
         pairs.one(
             lambda row: by_group[row].astype(jnp.float32) + far[row].astype(jnp.float32),
-            GROUP + 1 + turn, turn, sums[turn % len(sums)], first,
+            kepts[LEFT + turn], sums[turn], first,
         )
-    pairs.finish(2)
+        pairs.send(kepts[LEFT + turn], LEFT + turn, GROUP + 1 + turn)
+    pairs.finish(kepts)
 
 
 def moved(shard, pairs):
@@ -174,7 +185,8 @@
     slab = slc[:, 0] * valid_rows.astype(jnp.bfloat16)[0][None, :, None]
     slab = slab.reshape(2, height, blocks, BLOCK).transpose(1, 0, 2, 3).reshape(height, cells, BLOCK)
     slab = jnp.where(core == 0, slab, slab[::-1])
-    halo = lax.ppermute(slab[height - HALO :][::-1], "row", [(0, 1), (1, 0)])
+    halos = lax.all_gather(slab[height - HALO :][::-1], "row")
+    halo = jnp.where(core == 0, halos[1], halos[0])
     own = jnp.concatenate([slab, halo], axis=0)
     eight = moved(own, [(i, i - GROUP) for i in range(GROUP, length)])
     ends = range(PLANE, length, PLANE)
@@ -195,48 +207,50 @@
     )
     kept = jax.ShapeDtypeStruct((blocks, height, BLOCK), jnp.float32)
 
-    def scratch(turns, buffers):
+    def scratch(turns, copies):
         return [
             pltpu.SMEM((band,), jnp.int32),
-            pltpu.VMEM((rows, cells, BLOCK), jnp.float32),
-            pltpu.VMEM((3 * BLOCK, 2 * BLOCK), jnp.bfloat16),
             pltpu.VMEM((turns, 3, height, width), jnp.bfloat16),
-            pltpu.SemaphoreType.DMA((turns, 2)),
-        ] + [pltpu.VMEM((3, blocks * height, BLOCK), jnp.float32) for _ in range(buffers)]
+            pltpu.SemaphoreType.DMA((copies, 2)),
+        ] + [pltpu.VMEM((3, blocks * height, BLOCK), jnp.float32) for _ in range(2)]
 
     def cost(count):
         return pl.CostEstimate(flops=count << 33, bytes_accessed=count << 23, transcendentals=count << 15)
 
     params = pltpu.CompilerParams(vmem_limit_bytes=16 << 20)
-    phase, coher, first = pl.pallas_call(
+    handed = (
+        jax.ShapeDtypeStruct((rows, cells, BLOCK), jnp.float32),
+        jax.ShapeDtypeStruct((3 * BLOCK, 2 * BLOCK), jnp.bfloat16),
+    )
+    phase, coher, first, mine, ones = pl.pallas_call(
         first_kernel,
-        out_shape=outs + (kept,),
+        out_shape=outs + (kept,) + handed,
         in_specs=[SCALARS, SCALARS, WHOLE, WHOLE, AWAY, AWAY],
-        out_specs=(AWAY, AWAY, WHOLE),
-        scratch_shapes=scratch(1, 2),
+        out_specs=(AWAY, AWAY, WHOLE, WHOLE, WHOLE),
+        scratch_shapes=scratch(1, 1),
         compiler_params=params,
         cost_estimate=cost(3),
     )(pair_order, place, own, eight, nine_far, ten_far)
-    phase, coher = pl.pallas_call(
+    phase, coher, left = pl.pallas_call(
         near_kernel,
-        out_shape=outs,
-        in_specs=[SCALARS, SCALARS, WHOLE, WHOLE, WHOLE, AWAY, AWAY],
-        out_specs=(AWAY, AWAY),
-        scratch_shapes=scratch(GROUP - 1, 2),
-        input_output_aliases={5: 0, 6: 1},
+        out_shape=outs + (jax.ShapeDtypeStruct((LEFT, 3, height, width), jnp.bfloat16),),
+        in_specs=[SCALARS, SCALARS] + [WHOLE] * 4 + [AWAY, AWAY],
+        out_specs=(AWAY, AWAY, WHOLE),
+        scratch_shapes=scratch(GROUP - 1 - LEFT, GROUP - 1 - LEFT),
+        input_output_aliases={6: 0, 7: 1},
         compiler_params=params,
         cost_estimate=cost(GROUP - 1),
-    )(pair_order, place, own, near, first, phase, coher)
+    )(pair_order, place, near, first, mine, ones, phase, coher)
     phase, coher = pl.pallas_call(
         last_kernel,
         out_shape=outs,
-        in_specs=[SCALARS, SCALARS] + [WHOLE] * 6 + [AWAY, AWAY],
+        in_specs=[SCALARS, SCALARS] + [WHOLE] * 8 + [AWAY, AWAY],
         out_specs=(AWAY, AWAY),
-        scratch_shapes=scratch(2, 2),
-        input_output_aliases={8: 0, 9: 1},
+        scratch_shapes=scratch(2, LEFT + 2),
+        input_output_aliases={10: 0, 11: 1},
         compiler_params=params,
         cost_estimate=cost(2),
-    )(pair_order, place, own, nine, nine_far, ten, ten_far, first, phase, coher)
+    )(pair_order, place, left, nine, nine_far, ten, ten_far, first, mine, ones, phase, coher)
     return phase[:, None], coher[None]
 
 

time: 38.5 us -> 37.3 us (0.969)
  starting transfers between devices: 21.2 us -> 18.6 us
  blocking collectives: 0 us -> 2.17 us
  waiting for transfers between devices: 7.94 us -> 7.44 us
    ppermute x1 -> x0, starting transfers between devices: 2.58 us -> none  [shards(): halo = lax.ppermute(slab[height - HALO:][::-1], 'row', [(0, 1), (1, 0)])]
    all_gather x0 -> x1, blocking collectives: none -> 2.17 us  [shards(): halos = lax.all_gather(slab[height - HALO:][::-1], 'row')]
    ppermute x1 -> x0, waiting for transfers between devices: 0.79 us -> none  [shards(): halo = lax.ppermute(slab[height - HALO:][::-1], 'row', [(0, 1), (1, 0)])]
  transfers between devices with their start and end apart: 7 -> 6, of which waited for: 4 -> 3; matrix products, arithmetic and copies ran while one was open for 3% -> 3% of each run, Pallas kernels for 12% -> 11%
where the time goes in v4:
time: 37.3 us; the launch traced here: 36.9 us
  starting transfers between devices  18.6 us (50%)
  waiting for transfers between devices  7.44 us (20%)
  Pallas kernels  5.94 us (16%)
  blocking collectives  2.17 us (6%)
  other arithmetic  1.14 us (3%)
  local copies, waits for them, and re-layouts  0.87 us (2%)
  between operations  0.8 us (2%)
    ppermute x5, starting transfers between devices, moved(): return lax.ppermute(shard, 'date', pairs)  11.3 us
    all_to_all x1, starting transfers between devices, shards(): lax.all_to_all(given, 'date', 0, 0, axis_index_groups=groups, tiled=True)  7.32 us
    ppermute x5, waiting for transfers between devices, moved(): return lax.ppermute(shard, 'date', pairs)  5.43 us
    pallas_call x1, Pallas kernels, shards(): pl.pallas_call(near_kernel, out_shape=outs + (jax.ShapeDtypeStruct((LEFT,...  2.47 us
    all_gather x1, blocking collectives, shards(): halos = lax.all_gather(slab[height - HALO:][::-1], 'row')  2.17 us
    all_to_all x1, waiting for transfers between devices, shards(): lax.all_to_all(given, 'date', 0, 0, axis_index_groups=groups, tiled=True)  2.01 us
    pallas_call x1, Pallas kernels, shards(): pl.pallas_call(last_kernel, out_shape=outs, in_specs=[SCALARS, SCALARS] +...  1.85 us
    pallas_call x1, Pallas kernels, shards(): pl.pallas_call(first_kernel, out_shape=outs + (kept,) + handed, in_specs=...  1.62 us
  transfers between devices with their start and end apart: 6, of which 3 were waited for; matrix products, arithmetic and copies ran while one was open for 3% of the time, Pallas kernels for 11%

profile of v4, /device:TPU:251, one launch (start us, length us, event | category | flops | bytes accessed | tf_op | source)
XLA Modules:
  0.0 36.9 jit_solution(875424680771966536)
XLA Ops:
  0.6 0.0 copy-start.1
  0.6 0.9 %copy.13 = bf16[4,8,8,128]{3,2,1,0:T(8,128)(2,1)S(1)} copy(bf16[4,8,8,128]{3,1,2,0:T(8,128)(2,1)} %bitcast.22) | data formatting | bytes 131072
  1.5 0.0 copy-done.1
  1.5 0.1 fusion
  1.7 2.2 %all-gather = bf16[6,16,128]{2,1,0:T(8,128)(2,1)S(1)} all-gather(bf16[3,16,128]{2,1,0:T(8,128)(2,1)S(1)} %rev.7), channel_id=2, replica_groups=mesh['date'=256,'row'=2] {'row'}, dimensions={0}, use_global_device_ids=true | all-gather | bytes 36864 | tf_op jit(solution)/shard_map/all_gather | solution.py:188
  3.9 3.8 %collective-permute-start = (bf16[19,16,128]{2,1,0:T(8,128)(2,1)S(1)}, bf16[19,16,128]{2,1,0:T(8,128)(2,1)S(1)}, u32[]{:S(2)}, u32[]{:S(2)}) collective-permute-start(bf16[19,16,128]{2,1,0:T(8,128)(2,1)S(1)} %pad_maximum_fusion.own), channel_id=1, source_target_pairs={{16,0},{18,2},{20,4},{22,6},{24,8},{26,10},{28,12},{30,14},{32,16}... | collective-permute-start | bytes 233480 | tf_op jit(solution)/shard_map/ppermute | solution.py:173
  7.6 0.7 %collective-permute-start.1 = (bf16[19,16,128]{2,1,0:T(8,128)(2,1)S(1)}, bf16[19,16,128]{2,1,0:T(8,128)(2,1)S(1)}, u32[]{:S(2)}, u32[]{:S(2)}) collective-permute-start(bf16[19,16,128]{2,1,0:T(8,128)(2,1)S(1)} %pad_maximum_fusion.own), channel_id=1, source_target_pairs={{80,62},{144,126},{208,190},{272,254},{336,318},{400,382},{464,446... | collective-permute-start | bytes 233480 | tf_op jit(solution)/shard_map/ppermute | solution.py:173
  8.3 0.7 %collective-permute-start.2 = (bf16[19,16,128]{2,1,0:T(8,128)(2,1)S(1)}, bf16[19,16,128]{2,1,0:T(8,128)(2,1)S(1)}, u32[]{:S(2)}, u32[]{:S(2)}) collective-permute-start(bf16[19,16,128]{2,1,0:T(8,128)(2,1)S(1)} %pad_maximum_fusion.own), channel_id=1, source_target_pairs={{80,60},{82,62},{144,124},{146,126},{208,188},{210,190},{272,252},... | collective-permute-start | bytes 233480 | tf_op jit(solution)/shard_map/ppermute | solution.py:173
  9.0 0.1 pad_add_fusion.place
  9.1 4.6 %collective-permute-done.eight = bf16[19,16,128]{2,1,0:T(8,128)(2,1)S(1)} collective-permute-done((bf16[19,16,128]{2,1,0:T(8,128)(2,1)S(1)}, bf16[19,16,128]{2,1,0:T(8,128)(2,1)S(1)}, u32[]{:S(2)}, u32[]{:S(2)}) %collective-permute-start) | collective-permute-done | bytes 77856 | tf_op jit(solution)/shard_map/ppermute | solution.py:173
  13.6 0.9 %broadcast_select_fusion = bf16[8,19,16,128]{3,2,1,0:T(8,128)(2,1)} fusion(pred[8]{0:T(512)(128)(4,1)S(1)} %iota_compare_fusion, bf16[19,16,128]{2,1,0:T(8,128)(2,1)S(1)} %collective-permute-done.eight, bf16[19,16,128]{2,1,0:T(8,128)(2,1)S(1)} %pad_maximum_fusion.own), kind=kLoop, calls=%fused_computation | loop fusion | flops 311296 | bytes 778248 | tf_op jit(solution)/shard_map/jit(_where)/select_n | solution.py:196
  14.6 0.0 copy-start
  14.6 7.3 %all-to-all-start = ((bf16[8,19,16,128]{3,2,1,0:T(8,128)(2,1)}), bf16[8,19,16,128]{3,2,1,0:T(8,128)(2,1)S(1)}, u32[]{:S(2)}, u32[]{:S(2)}) async-start(bf16[8,19,16,128]{3,2,1,0:T(8,128)(2,1)} %broadcast_select_fusion), calls=%async_computation | async-start | bytes 1245184 | tf_op jit(solution)/shard_map/all_to_all | solution.py:198
  21.9 2.2 %collective-permute-start.3 = (bf16[19,16,128]{2,1,0:T(8,128)(2,1)S(1)}, bf16[19,16,128]{2,1,0:T(8,128)(2,1)S(1)}, u32[]{:S(2)}, u32[]{:S(2)}) collective-permute-start(bf16[19,16,128]{2,1,0:T(8,128)(2,1)S(1)} %collective-permute-done.eight), channel_id=1, source_target_pairs={{2,0},{4,2},{6,4},{8,6},{10,8},{12,10},{14,12},{16,14},{18,16},{20... | collective-permute-start | bytes 233480 | tf_op jit(solution)/shard_map/ppermute | solution.py:173
  24.1 4.0 %collective-permute-start.4 = (bf16[19,16,128]{2,1,0:T(8,128)(2,1)S(1)}, bf16[19,16,128]{2,1,0:T(8,128)(2,1)S(1)}, u32[]{:S(2)}, u32[]{:S(2)}) collective-permute-start(bf16[19,16,128]{2,1,0:T(8,128)(2,1)S(1)} %collective-permute-done.eight), channel_id=1, source_target_pairs={{4,0},{6,2},{8,4},{10,6},{12,8},{14,10},{16,12},{18,14},{20,16},{2... | collective-permute-start | bytes 233480 | tf_op jit(solution)/shard_map/ppermute | solution.py:173
  28.1 0.0 collective-permute-done.1._n.nine_far
  28.1 0.0 collective-permute-done.2._t.ten_far
  28.1 0.0 copy-done
  28.1 1.6 %shard_map.50 = (bf16[2,10,16,1024]{3,2,1,0:T(8,128)(2,1)}, bf16[10,16,1024]{2,1,0:T(8,128)(2,1)}, f32[8,16,128]{2,1,0:T(8,128)S(1)}, f32[19,16,128]{2,1,0:T(8,128)S(1)}, bf16[384,256]{1,0:T(8,128)(2,1)S(1)}) custom-call(s32[1,10]{1,0:T(1,128)S(1)} %copy-done, s32[2]{0:T(128)S(1)} %pad_add_fusion.place, bf16[19,16,128]{2,1,0:T(8,128)(2,1)S(1)} %pad_maximum_fusion.own, ...), custom_call_target="tpu_custom_call" | custom-call | flops 25769803776 | bytes 25165824 | tf_op jit(solution)/shard_map/pallas_call | solution.py:225
  29.7 2.0 %all-to-all-done.near = bf16[8,19,16,128]{3,2,1,0:T(8,128)(2,1)S(1)} async-done(((bf16[8,19,16,128]{3,2,1,0:T(8,128)(2,1)}), bf16[8,19,16,128]{3,2,1,0:T(8,128)(2,1)S(1)}, u32[]{:S(2)}, u32[]{:S(2)}) %all-to-all-start) | async-done | bytes 622624 | tf_op jit(solution)/shard_map/all_to_all | solution.py:198
  31.8 2.5 %shard_map.51 = (bf16[2,10,16,1024]{3,2,1,0:T(8,128)(2,1)}, bf16[10,16,1024]{2,1,0:T(8,128)(2,1)}, bf16[3,3,16,1024]{3,2,1,0:T(8,128)(2,1)S(1)}) custom-call(s32[1,10]{1,0:T(1,128)S(1)} %copy-done, s32[2]{0:T(128)S(1)} %pad_add_fusion.place, bf16[8,19,16,128]{3,2,1,0:T(8,128)(2,1)S(1)} %all-to-all-done.near, ...), custom_call_target="tpu_custom_call", output_to_operand_aliasing={{0}: (6, {}), {1}: (7, {})} | custom-call | flops 60129542144 | bytes 58720256 | tf_op jit(solution)/shard_map/pallas_call | solution.py:234
  34.2 0.0 collective-permute-done.3.nine
  34.2 0.9 %collective-permute-done.4.ten = bf16[19,16,128]{2,1,0:T(8,128)(2,1)S(1)} collective-permute-done((bf16[19,16,128]{2,1,0:T(8,128)(2,1)S(1)}, bf16[19,16,128]{2,1,0:T(8,128)(2,1)S(1)}, u32[]{:S(2)}, u32[]{:S(2)}) %collective-permute-start.4) | collective-permute-done | bytes 77856 | tf_op jit(solution)/shard_map/ppermute | solution.py:173
  35.1 1.9 %shard_map.52 = (bf16[2,10,16,1024]{3,2,1,0:T(8,128)(2,1)}, bf16[10,16,1024]{2,1,0:T(8,128)(2,1)}) custom-call(s32[1,10]{1,0:T(1,128)S(1)} %copy-done, s32[2]{0:T(128)S(1)} %pad_add_fusion.place, bf16[3,3,16,1024]{3,2,1,0:T(8,128)(2,1)S(1)} %get-tuple-element.17.left, ...), custom_call_target="tpu_custom_call", output_to_operand_aliasing={{0}: (10, {}), {1}: (11, {})} | custom-call | flops 17179869184 | bytes 16777216 | tf_op jit(solution)/shard_map/pallas_call | solution.py:244
  (7 shorter events, 0.0 us)
Async XLA Ops:
  0.6 0.9 %copy-start.1 = (s32[1,16]{1,0:T(1,128)S(1)}, s32[1,16]{1,0:T(1,128)}, u32[]{:S(2)}) copy-start(s32[1,16]{1,0:T(1,128)} %param.4) | copy-start | bytes 196
  3.9 9.8 %collective-permute-start = (bf16[19,16,128]{2,1,0:T(8,128)(2,1)S(1)}, bf16[19,16,128]{2,1,0:T(8,128)(2,1)S(1)}, u32[]{:S(2)}, u32[]{:S(2)}) collective-permute-start(bf16[19,16,128]{2,1,0:T(8,128)(2,1)S(1)} %pad_maximum_fusion.own), channel_id=1, source_target_pairs={{16,0},{18,2},{20,4},{22,6},{24,8},{26,10},{28,12},{30,14},{32,16}... | collective-permute-start | bytes 233480 | tf_op jit(solution)/shard_map/ppermute | solution.py:173
  7.6 20.5 %collective-permute-start.1 = (bf16[19,16,128]{2,1,0:T(8,128)(2,1)S(1)}, bf16[19,16,128]{2,1,0:T(8,128)(2,1)S(1)}, u32[]{:S(2)}, u32[]{:S(2)}) collective-permute-start(bf16[19,16,128]{2,1,0:T(8,128)(2,1)S(1)} %pad_maximum_fusion.own), channel_id=1, source_target_pairs={{80,62},{144,126},{208,190},{272,254},{336,318},{400,382},{464,446... | collective-permute-start | bytes 233480 | tf_op jit(solution)/shard_map/ppermute | solution.py:173
  8.3 19.8 %collective-permute-start.2 = (bf16[19,16,128]{2,1,0:T(8,128)(2,1)S(1)}, bf16[19,16,128]{2,1,0:T(8,128)(2,1)S(1)}, u32[]{:S(2)}, u32[]{:S(2)}) collective-permute-start(bf16[19,16,128]{2,1,0:T(8,128)(2,1)S(1)} %pad_maximum_fusion.own), channel_id=1, source_target_pairs={{80,60},{82,62},{144,124},{146,126},{208,188},{210,190},{272,252},... | collective-permute-start | bytes 233480 | tf_op jit(solution)/shard_map/ppermute | solution.py:173
  14.6 13.5 %copy-start = (s32[1,10]{1,0:T(1,128)S(1)}, s32[1,10]{1,0:T(1,128)}, u32[]{:S(2)}) copy-start(s32[1,10]{1,0:T(1,128)} %order.5) | copy-start | bytes 124
  14.6 17.2 %all-to-all-start = ((bf16[8,19,16,128]{3,2,1,0:T(8,128)(2,1)}), bf16[8,19,16,128]{3,2,1,0:T(8,128)(2,1)S(1)}, u32[]{:S(2)}, u32[]{:S(2)}) async-start(bf16[8,19,16,128]{3,2,1,0:T(8,128)(2,1)} %broadcast_select_fusion), calls=%async_computation | async-start | bytes 1245184 | tf_op jit(solution)/shard_map/all_to_all | solution.py:198
  21.9 12.3 %collective-permute-start.3 = (bf16[19,16,128]{2,1,0:T(8,128)(2,1)S(1)}, bf16[19,16,128]{2,1,0:T(8,128)(2,1)S(1)}, u32[]{:S(2)}, u32[]{:S(2)}) collective-permute-start(bf16[19,16,128]{2,1,0:T(8,128)(2,1)S(1)} %collective-permute-done.eight), channel_id=1, source_target_pairs={{2,0},{4,2},{6,4},{8,6},{10,8},{12,10},{14,12},{16,14},{18,16},{20... | collective-permute-start | bytes 233480 | tf_op jit(solution)/shard_map/ppermute | solution.py:173
  24.1 11.0 %collective-permute-start.4 = (bf16[19,16,128]{2,1,0:T(8,128)(2,1)S(1)}, bf16[19,16,128]{2,1,0:T(8,128)(2,1)S(1)}, u32[]{:S(2)}, u32[]{:S(2)}) collective-permute-start(bf16[19,16,128]{2,1,0:T(8,128)(2,1)S(1)} %collective-permute-done.eight), channel_id=1, source_target_pairs={{4,0},{6,2},{8,4},{10,6},{12,8},{14,10},{16,12},{18,14},{20,16},{2... | collective-permute-start | bytes 233480 | tf_op jit(solution)/shard_map/ppermute | solution.py:173

commit v5 on v4

--- a/solution.py
+++ b/solution.py
@@ -7,7 +7,7 @@
 
 GROUP = 8
 PLANE = 32
-LEFT = 3
+LEFT = 5
 HALO = 3
 BLOCK = 128
 TINY = 1.1754944e-38
@@ -165,6 +165,7 @@
             lambda row: by_group[row].astype(jnp.float32) + far[row].astype(jnp.float32),
             kepts[LEFT + turn], sums[turn], first,
         )
+    for turn in range(2):
         pairs.send(kepts[LEFT + turn], LEFT + turn, GROUP + 1 + turn)
     pairs.finish(kepts)
 

time: 37.3 us -> 37.3 us (level)
  transfers between devices with their start and end apart: 6 -> 6, of which waited for: 3 -> 3; matrix products, arithmetic and copies ran while one was open for 3% -> 3% of each run, Pallas kernels for 11% -> 10%
where the time goes in v5:
time: 37.3 us; the launch traced here: 37 us
  starting transfers between devices  18.6 us (50%)
  waiting for transfers between devices  7.65 us (21%)
  Pallas kernels  5.76 us (15%)
  blocking collectives  2.17 us (6%)
  other arithmetic  1.14 us (3%)
  local copies, waits for them, and re-layouts  0.87 us (2%)
  between operations  0.8 us (2%)
    ppermute x5, starting transfers between devices, moved(): return lax.ppermute(shard, 'date', pairs)  11.3 us
    all_to_all x1, starting transfers between devices, shards(): lax.all_to_all(given, 'date', 0, 0, axis_index_groups=groups, tiled=True)  7.32 us
    ppermute x5, waiting for transfers between devices, moved(): return lax.ppermute(shard, 'date', pairs)  5.64 us
    pallas_call x1, Pallas kernels, shards(): pl.pallas_call(near_kernel, out_shape=outs + (jax.ShapeDtypeStruct((LEFT,...  2.25 us
    all_gather x1, blocking collectives, shards(): halos = lax.all_gather(slab[height - HALO:][::-1], 'row')  2.17 us
    all_to_all x1, waiting for transfers between devices, shards(): lax.all_to_all(given, 'date', 0, 0, axis_index_groups=groups, tiled=True)  2.01 us
    pallas_call x1, Pallas kernels, shards(): pl.pallas_call(last_kernel, out_shape=outs, in_specs=[SCALARS, SCALARS] +...  1.89 us
    pallas_call x1, Pallas kernels, shards(): pl.pallas_call(first_kernel, out_shape=outs + (kept,) + handed, in_specs=...  1.62 us
  transfers between devices with their start and end apart: 6, of which 3 were waited for; matrix products, arithmetic and copies ran while one was open for 3% of the time, Pallas kernels for 10%

profile of v5, /device:TPU:251, one launch (start us, length us, event | category | flops | bytes accessed | tf_op | source)
XLA Modules:
  0.0 37.0 jit_solution(1764592227758868002)
XLA Ops:
  0.6 0.0 copy-start.1
  0.6 0.9 %copy.13 = bf16[4,8,8,128]{3,2,1,0:T(8,128)(2,1)S(1)} copy(bf16[4,8,8,128]{3,1,2,0:T(8,128)(2,1)} %bitcast.22) | data formatting | bytes 131072
  1.5 0.0 copy-done.1
  1.5 0.1 fusion
  1.7 2.2 %all-gather = bf16[6,16,128]{2,1,0:T(8,128)(2,1)S(1)} all-gather(bf16[3,16,128]{2,1,0:T(8,128)(2,1)S(1)} %rev.7), channel_id=2, replica_groups=mesh['date'=256,'row'=2] {'row'}, dimensions={0}, use_global_device_ids=true | all-gather | bytes 36864 | tf_op jit(solution)/shard_map/all_gather | solution.py:189
  3.9 3.8 %collective-permute-start = (bf16[19,16,128]{2,1,0:T(8,128)(2,1)S(1)}, bf16[19,16,128]{2,1,0:T(8,128)(2,1)S(1)}, u32[]{:S(2)}, u32[]{:S(2)}) collective-permute-start(bf16[19,16,128]{2,1,0:T(8,128)(2,1)S(1)} %pad_maximum_fusion.own), channel_id=1, source_target_pairs={{16,0},{18,2},{20,4},{22,6},{24,8},{26,10},{28,12},{30,14},{32,16}... | collective-permute-start | bytes 233480 | tf_op jit(solution)/shard_map/ppermute | solution.py:174
  7.6 0.7 %collective-permute-start.1 = (bf16[19,16,128]{2,1,0:T(8,128)(2,1)S(1)}, bf16[19,16,128]{2,1,0:T(8,128)(2,1)S(1)}, u32[]{:S(2)}, u32[]{:S(2)}) collective-permute-start(bf16[19,16,128]{2,1,0:T(8,128)(2,1)S(1)} %pad_maximum_fusion.own), channel_id=1, source_target_pairs={{80,62},{144,126},{208,190},{272,254},{336,318},{400,382},{464,446... | collective-permute-start | bytes 233480 | tf_op jit(solution)/shard_map/ppermute | solution.py:174
  8.3 0.7 %collective-permute-start.2 = (bf16[19,16,128]{2,1,0:T(8,128)(2,1)S(1)}, bf16[19,16,128]{2,1,0:T(8,128)(2,1)S(1)}, u32[]{:S(2)}, u32[]{:S(2)}) collective-permute-start(bf16[19,16,128]{2,1,0:T(8,128)(2,1)S(1)} %pad_maximum_fusion.own), channel_id=1, source_target_pairs={{80,60},{82,62},{144,124},{146,126},{208,188},{210,190},{272,252},... | collective-permute-start | bytes 233480 | tf_op jit(solution)/shard_map/ppermute | solution.py:174
  9.0 0.1 pad_add_fusion.place
  9.1 4.6 %collective-permute-done.eight = bf16[19,16,128]{2,1,0:T(8,128)(2,1)S(1)} collective-permute-done((bf16[19,16,128]{2,1,0:T(8,128)(2,1)S(1)}, bf16[19,16,128]{2,1,0:T(8,128)(2,1)S(1)}, u32[]{:S(2)}, u32[]{:S(2)}) %collective-permute-start) | collective-permute-done | bytes 77856 | tf_op jit(solution)/shard_map/ppermute | solution.py:174
  13.6 0.9 %broadcast_select_fusion = bf16[8,19,16,128]{3,2,1,0:T(8,128)(2,1)} fusion(pred[8]{0:T(512)(128)(4,1)S(1)} %iota_compare_fusion, bf16[19,16,128]{2,1,0:T(8,128)(2,1)S(1)} %collective-permute-done.eight, bf16[19,16,128]{2,1,0:T(8,128)(2,1)S(1)} %pad_maximum_fusion.own), kind=kLoop, calls=%fused_computation | loop fusion | flops 311296 | bytes 778248 | tf_op jit(solution)/shard_map/jit(_where)/select_n | solution.py:197
  14.6 0.0 copy-start
  14.6 7.3 %all-to-all-start = ((bf16[8,19,16,128]{3,2,1,0:T(8,128)(2,1)}), bf16[8,19,16,128]{3,2,1,0:T(8,128)(2,1)S(1)}, u32[]{:S(2)}, u32[]{:S(2)}) async-start(bf16[8,19,16,128]{3,2,1,0:T(8,128)(2,1)} %broadcast_select_fusion), calls=%async_computation | async-start | bytes 1245184 | tf_op jit(solution)/shard_map/all_to_all | solution.py:199
  21.9 2.2 %collective-permute-start.3 = (bf16[19,16,128]{2,1,0:T(8,128)(2,1)S(1)}, bf16[19,16,128]{2,1,0:T(8,128)(2,1)S(1)}, u32[]{:S(2)}, u32[]{:S(2)}) collective-permute-start(bf16[19,16,128]{2,1,0:T(8,128)(2,1)S(1)} %collective-permute-done.eight), channel_id=1, source_target_pairs={{2,0},{4,2},{6,4},{8,6},{10,8},{12,10},{14,12},{16,14},{18,16},{20... | collective-permute-start | bytes 233480 | tf_op jit(solution)/shard_map/ppermute | solution.py:174
  24.1 4.0 %collective-permute-start.4 = (bf16[19,16,128]{2,1,0:T(8,128)(2,1)S(1)}, bf16[19,16,128]{2,1,0:T(8,128)(2,1)S(1)}, u32[]{:S(2)}, u32[]{:S(2)}) collective-permute-start(bf16[19,16,128]{2,1,0:T(8,128)(2,1)S(1)} %collective-permute-done.eight), channel_id=1, source_target_pairs={{4,0},{6,2},{8,4},{10,6},{12,8},{14,10},{16,12},{18,14},{20,16},{2... | collective-permute-start | bytes 233480 | tf_op jit(solution)/shard_map/ppermute | solution.py:174
  28.1 0.0 collective-permute-done.1._n.nine_far
  28.1 0.0 collective-permute-done.2._t.ten_far
  28.1 0.0 copy-done
  28.1 1.6 %shard_map.50 = (bf16[2,10,16,1024]{3,2,1,0:T(8,128)(2,1)}, bf16[10,16,1024]{2,1,0:T(8,128)(2,1)}, f32[8,16,128]{2,1,0:T(8,128)S(1)}, f32[19,16,128]{2,1,0:T(8,128)S(1)}, bf16[384,256]{1,0:T(8,128)(2,1)S(1)}) custom-call(s32[1,10]{1,0:T(1,128)S(1)} %copy-done, s32[2]{0:T(128)S(1)} %pad_add_fusion.place, bf16[19,16,128]{2,1,0:T(8,128)(2,1)S(1)} %pad_maximum_fusion.own, ...), custom_call_target="tpu_custom_call" | custom-call | flops 25769803776 | bytes 25165824 | tf_op jit(solution)/shard_map/pallas_call | solution.py:226
  29.7 2.0 %all-to-all-done.near = bf16[8,19,16,128]{3,2,1,0:T(8,128)(2,1)S(1)} async-done(((bf16[8,19,16,128]{3,2,1,0:T(8,128)(2,1)}), bf16[8,19,16,128]{3,2,1,0:T(8,128)(2,1)S(1)}, u32[]{:S(2)}, u32[]{:S(2)}) %all-to-all-start) | async-done | bytes 622624 | tf_op jit(solution)/shard_map/all_to_all | solution.py:199
  31.8 2.3 %shard_map.51 = (bf16[2,10,16,1024]{3,2,1,0:T(8,128)(2,1)}, bf16[10,16,1024]{2,1,0:T(8,128)(2,1)}, bf16[5,3,16,1024]{3,2,1,0:T(8,128)(2,1)S(1)}) custom-call(s32[1,10]{1,0:T(1,128)S(1)} %copy-done, s32[2]{0:T(128)S(1)} %pad_add_fusion.place, bf16[8,19,16,128]{3,2,1,0:T(8,128)(2,1)S(1)} %all-to-all-done.near, ...), custom_call_target="tpu_custom_call", output_to_operand_aliasing={{0}: (6, {}), {1}: (7, {})} | custom-call | flops 60129542144 | bytes 58720256 | tf_op jit(solution)/shard_map/pallas_call | solution.py:235
  34.0 0.0 collective-permute-done.3.nine
  34.0 1.1 %collective-permute-done.4.ten = bf16[19,16,128]{2,1,0:T(8,128)(2,1)S(1)} collective-permute-done((bf16[19,16,128]{2,1,0:T(8,128)(2,1)S(1)}, bf16[19,16,128]{2,1,0:T(8,128)(2,1)S(1)}, u32[]{:S(2)}, u32[]{:S(2)}) %collective-permute-start.4) | collective-permute-done | bytes 77856 | tf_op jit(solution)/shard_map/ppermute | solution.py:174
  35.1 1.9 %shard_map.52 = (bf16[2,10,16,1024]{3,2,1,0:T(8,128)(2,1)}, bf16[10,16,1024]{2,1,0:T(8,128)(2,1)}) custom-call(s32[1,10]{1,0:T(1,128)S(1)} %copy-done, s32[2]{0:T(128)S(1)} %pad_add_fusion.place, bf16[5,3,16,1024]{3,2,1,0:T(8,128)(2,1)S(1)} %get-tuple-element.17.left, ...), custom_call_target="tpu_custom_call", output_to_operand_aliasing={{0}: (10, {}), {1}: (11, {})} | custom-call | flops 17179869184 | bytes 16777216 | tf_op jit(solution)/shard_map/pallas_call | solution.py:245
  (7 shorter events, 0.0 us)
Async XLA Ops:
  0.6 0.9 %copy-start.1 = (s32[1,16]{1,0:T(1,128)S(1)}, s32[1,16]{1,0:T(1,128)}, u32[]{:S(2)}) copy-start(s32[1,16]{1,0:T(1,128)} %param.4) | copy-start | bytes 196
  3.9 9.8 %collective-permute-start = (bf16[19,16,128]{2,1,0:T(8,128)(2,1)S(1)}, bf16[19,16,128]{2,1,0:T(8,128)(2,1)S(1)}, u32[]{:S(2)}, u32[]{:S(2)}) collective-permute-start(bf16[19,16,128]{2,1,0:T(8,128)(2,1)S(1)} %pad_maximum_fusion.own), channel_id=1, source_target_pairs={{16,0},{18,2},{20,4},{22,6},{24,8},{26,10},{28,12},{30,14},{32,16}... | collective-permute-start | bytes 233480 | tf_op jit(solution)/shard_map/ppermute | solution.py:174
  7.6 20.5 %collective-permute-start.1 = (bf16[19,16,128]{2,1,0:T(8,128)(2,1)S(1)}, bf16[19,16,128]{2,1,0:T(8,128)(2,1)S(1)}, u32[]{:S(2)}, u32[]{:S(2)}) collective-permute-start(bf16[19,16,128]{2,1,0:T(8,128)(2,1)S(1)} %pad_maximum_fusion.own), channel_id=1, source_target_pairs={{80,62},{144,126},{208,190},{272,254},{336,318},{400,382},{464,446... | collective-permute-start | bytes 233480 | tf_op jit(solution)/shard_map/ppermute | solution.py:174
  8.3 19.8 %collective-permute-start.2 = (bf16[19,16,128]{2,1,0:T(8,128)(2,1)S(1)}, bf16[19,16,128]{2,1,0:T(8,128)(2,1)S(1)}, u32[]{:S(2)}, u32[]{:S(2)}) collective-permute-start(bf16[19,16,128]{2,1,0:T(8,128)(2,1)S(1)} %pad_maximum_fusion.own), channel_id=1, source_target_pairs={{80,60},{82,62},{144,124},{146,126},{208,188},{210,190},{272,252},... | collective-permute-start | bytes 233480 | tf_op jit(solution)/shard_map/ppermute | solution.py:174
  14.6 13.5 %copy-start = (s32[1,10]{1,0:T(1,128)S(1)}, s32[1,10]{1,0:T(1,128)}, u32[]{:S(2)}) copy-start(s32[1,10]{1,0:T(1,128)} %order.5) | copy-start | bytes 124
  14.6 17.2 %all-to-all-start = ((bf16[8,19,16,128]{3,2,1,0:T(8,128)(2,1)}), bf16[8,19,16,128]{3,2,1,0:T(8,128)(2,1)S(1)}, u32[]{:S(2)}, u32[]{:S(2)}) async-start(bf16[8,19,16,128]{3,2,1,0:T(8,128)(2,1)} %broadcast_select_fusion), calls=%async_computation | async-start | bytes 1245184 | tf_op jit(solution)/shard_map/all_to_all | solution.py:199
  21.9 12.1 %collective-permute-start.3 = (bf16[19,16,128]{2,1,0:T(8,128)(2,1)S(1)}, bf16[19,16,128]{2,1,0:T(8,128)(2,1)S(1)}, u32[]{:S(2)}, u32[]{:S(2)}) collective-permute-start(bf16[19,16,128]{2,1,0:T(8,128)(2,1)S(1)} %collective-permute-done.eight), channel_id=1, source_target_pairs={{2,0},{4,2},{6,4},{8,6},{10,8},{12,10},{14,12},{16,14},{18,16},{20... | collective-permute-start | bytes 233480 | tf_op jit(solution)/shard_map/ppermute | solution.py:174
  24.1 11.0 %collective-permute-start.4 = (bf16[19,16,128]{2,1,0:T(8,128)(2,1)S(1)}, bf16[19,16,128]{2,1,0:T(8,128)(2,1)S(1)}, u32[]{:S(2)}, u32[]{:S(2)}) collective-permute-start(bf16[19,16,128]{2,1,0:T(8,128)(2,1)S(1)} %collective-permute-done.eight), channel_id=1, source_target_pairs={{4,0},{6,2},{8,4},{10,6},{12,8},{14,10},{16,12},{18,14},{20,16},{2... | collective-permute-start | bytes 233480 | tf_op jit(solution)/shard_map/ppermute | solution.py:174

commit v6 on v4

--- a/solution.py
+++ b/solution.py
@@ -165,6 +165,7 @@
             lambda row: by_group[row].astype(jnp.float32) + far[row].astype(jnp.float32),
             kepts[LEFT + turn], sums[turn], first,
         )
+    for turn in range(2):
         pairs.send(kepts[LEFT + turn], LEFT + turn, GROUP + 1 + turn)
     pairs.finish(kepts)
 

time: 37.3 us -> 37.3 us (level)
  no operation moved by 1% of the time
where the time goes in v6:
time: 37.3 us; the launch traced here: 36.9 us
  starting transfers between devices  18.6 us (50%)
  waiting for transfers between devices  7.44 us (20%)
  Pallas kernels  5.94 us (16%)
  blocking collectives  2.17 us (6%)
  other arithmetic  1.14 us (3%)
  local copies, waits for them, and re-layouts  0.87 us (2%)
  between operations  0.8 us (2%)
    ppermute x5, starting transfers between devices, moved(): return lax.ppermute(shard, 'date', pairs)  11.3 us
    all_to_all x1, starting transfers between devices, shards(): lax.all_to_all(given, 'date', 0, 0, axis_index_groups=groups, tiled=True)  7.32 us
    ppermute x5, waiting for transfers between devices, moved(): return lax.ppermute(shard, 'date', pairs)  5.43 us
    pallas_call x1, Pallas kernels, shards(): pl.pallas_call(near_kernel, out_shape=outs + (jax.ShapeDtypeStruct((LEFT,...  2.47 us
    all_gather x1, blocking collectives, shards(): halos = lax.all_gather(slab[height - HALO:][::-1], 'row')  2.17 us
    all_to_all x1, waiting for transfers between devices, shards(): lax.all_to_all(given, 'date', 0, 0, axis_index_groups=groups, tiled=True)  2.01 us
    pallas_call x1, Pallas kernels, shards(): pl.pallas_call(last_kernel, out_shape=outs, in_specs=[SCALARS, SCALARS] +...  1.85 us
    pallas_call x1, Pallas kernels, shards(): pl.pallas_call(first_kernel, out_shape=outs + (kept,) + handed, in_specs=...  1.62 us
  transfers between devices with their start and end apart: 6, of which 3 were waited for; matrix products, arithmetic and copies ran while one was open for 3% of the time, Pallas kernels for 11%

profile of v6, /device:TPU:251, one launch (start us, length us, event | category | flops | bytes accessed | tf_op | source)
XLA Modules:
  0.0 36.9 jit_solution(10222333378128681507)
XLA Ops:
  0.6 0.0 copy-start.1
  0.6 0.9 %copy.13 = bf16[4,8,8,128]{3,2,1,0:T(8,128)(2,1)S(1)} copy(bf16[4,8,8,128]{3,1,2,0:T(8,128)(2,1)} %bitcast.22) | data formatting | bytes 131072
  1.5 0.0 copy-done.1
  1.5 0.1 fusion
  1.7 2.2 %all-gather = bf16[6,16,128]{2,1,0:T(8,128)(2,1)S(1)} all-gather(bf16[3,16,128]{2,1,0:T(8,128)(2,1)S(1)} %rev.7), channel_id=2, replica_groups=mesh['date'=256,'row'=2] {'row'}, dimensions={0}, use_global_device_ids=true | all-gather | bytes 36864 | tf_op jit(solution)/shard_map/all_gather | solution.py:189
  3.9 3.8 %collective-permute-start = (bf16[19,16,128]{2,1,0:T(8,128)(2,1)S(1)}, bf16[19,16,128]{2,1,0:T(8,128)(2,1)S(1)}, u32[]{:S(2)}, u32[]{:S(2)}) collective-permute-start(bf16[19,16,128]{2,1,0:T(8,128)(2,1)S(1)} %pad_maximum_fusion.own), channel_id=1, source_target_pairs={{16,0},{18,2},{20,4},{22,6},{24,8},{26,10},{28,12},{30,14},{32,16}... | collective-permute-start | bytes 233480 | tf_op jit(solution)/shard_map/ppermute | solution.py:174
  7.6 0.7 %collective-permute-start.1 = (bf16[19,16,128]{2,1,0:T(8,128)(2,1)S(1)}, bf16[19,16,128]{2,1,0:T(8,128)(2,1)S(1)}, u32[]{:S(2)}, u32[]{:S(2)}) collective-permute-start(bf16[19,16,128]{2,1,0:T(8,128)(2,1)S(1)} %pad_maximum_fusion.own), channel_id=1, source_target_pairs={{80,62},{144,126},{208,190},{272,254},{336,318},{400,382},{464,446... | collective-permute-start | bytes 233480 | tf_op jit(solution)/shard_map/ppermute | solution.py:174
  8.3 0.7 %collective-permute-start.2 = (bf16[19,16,128]{2,1,0:T(8,128)(2,1)S(1)}, bf16[19,16,128]{2,1,0:T(8,128)(2,1)S(1)}, u32[]{:S(2)}, u32[]{:S(2)}) collective-permute-start(bf16[19,16,128]{2,1,0:T(8,128)(2,1)S(1)} %pad_maximum_fusion.own), channel_id=1, source_target_pairs={{80,60},{82,62},{144,124},{146,126},{208,188},{210,190},{272,252},... | collective-permute-start | bytes 233480 | tf_op jit(solution)/shard_map/ppermute | solution.py:174
  9.0 0.1 pad_add_fusion.place
  9.1 4.6 %collective-permute-done.eight = bf16[19,16,128]{2,1,0:T(8,128)(2,1)S(1)} collective-permute-done((bf16[19,16,128]{2,1,0:T(8,128)(2,1)S(1)}, bf16[19,16,128]{2,1,0:T(8,128)(2,1)S(1)}, u32[]{:S(2)}, u32[]{:S(2)}) %collective-permute-start) | collective-permute-done | bytes 77856 | tf_op jit(solution)/shard_map/ppermute | solution.py:174
  13.6 0.9 %broadcast_select_fusion = bf16[8,19,16,128]{3,2,1,0:T(8,128)(2,1)} fusion(pred[8]{0:T(512)(128)(4,1)S(1)} %iota_compare_fusion, bf16[19,16,128]{2,1,0:T(8,128)(2,1)S(1)} %collective-permute-done.eight, bf16[19,16,128]{2,1,0:T(8,128)(2,1)S(1)} %pad_maximum_fusion.own), kind=kLoop, calls=%fused_computation | loop fusion | flops 311296 | bytes 778248 | tf_op jit(solution)/shard_map/jit(_where)/select_n | solution.py:197
  14.6 0.0 copy-start
  14.6 7.3 %all-to-all-start = ((bf16[8,19,16,128]{3,2,1,0:T(8,128)(2,1)}), bf16[8,19,16,128]{3,2,1,0:T(8,128)(2,1)S(1)}, u32[]{:S(2)}, u32[]{:S(2)}) async-start(bf16[8,19,16,128]{3,2,1,0:T(8,128)(2,1)} %broadcast_select_fusion), calls=%async_computation | async-start | bytes 1245184 | tf_op jit(solution)/shard_map/all_to_all | solution.py:199
  21.9 2.2 %collective-permute-start.3 = (bf16[19,16,128]{2,1,0:T(8,128)(2,1)S(1)}, bf16[19,16,128]{2,1,0:T(8,128)(2,1)S(1)}, u32[]{:S(2)}, u32[]{:S(2)}) collective-permute-start(bf16[19,16,128]{2,1,0:T(8,128)(2,1)S(1)} %collective-permute-done.eight), channel_id=1, source_target_pairs={{2,0},{4,2},{6,4},{8,6},{10,8},{12,10},{14,12},{16,14},{18,16},{20... | collective-permute-start | bytes 233480 | tf_op jit(solution)/shard_map/ppermute | solution.py:174
  24.1 4.0 %collective-permute-start.4 = (bf16[19,16,128]{2,1,0:T(8,128)(2,1)S(1)}, bf16[19,16,128]{2,1,0:T(8,128)(2,1)S(1)}, u32[]{:S(2)}, u32[]{:S(2)}) collective-permute-start(bf16[19,16,128]{2,1,0:T(8,128)(2,1)S(1)} %collective-permute-done.eight), channel_id=1, source_target_pairs={{4,0},{6,2},{8,4},{10,6},{12,8},{14,10},{16,12},{18,14},{20,16},{2... | collective-permute-start | bytes 233480 | tf_op jit(solution)/shard_map/ppermute | solution.py:174
  28.1 0.0 collective-permute-done.1._n.nine_far
  28.1 0.0 collective-permute-done.2._t.ten_far
  28.1 0.0 copy-done
  28.1 1.6 %shard_map.50 = (bf16[2,10,16,1024]{3,2,1,0:T(8,128)(2,1)}, bf16[10,16,1024]{2,1,0:T(8,128)(2,1)}, f32[8,16,128]{2,1,0:T(8,128)S(1)}, f32[19,16,128]{2,1,0:T(8,128)S(1)}, bf16[384,256]{1,0:T(8,128)(2,1)S(1)}) custom-call(s32[1,10]{1,0:T(1,128)S(1)} %copy-done, s32[2]{0:T(128)S(1)} %pad_add_fusion.place, bf16[19,16,128]{2,1,0:T(8,128)(2,1)S(1)} %pad_maximum_fusion.own, ...), custom_call_target="tpu_custom_call" | custom-call | flops 25769803776 | bytes 25165824 | tf_op jit(solution)/shard_map/pallas_call | solution.py:226
  29.7 2.0 %all-to-all-done.near = bf16[8,19,16,128]{3,2,1,0:T(8,128)(2,1)S(1)} async-done(((bf16[8,19,16,128]{3,2,1,0:T(8,128)(2,1)}), bf16[8,19,16,128]{3,2,1,0:T(8,128)(2,1)S(1)}, u32[]{:S(2)}, u32[]{:S(2)}) %all-to-all-start) | async-done | bytes 622624 | tf_op jit(solution)/shard_map/all_to_all | solution.py:199
  31.8 2.5 %shard_map.51 = (bf16[2,10,16,1024]{3,2,1,0:T(8,128)(2,1)}, bf16[10,16,1024]{2,1,0:T(8,128)(2,1)}, bf16[3,3,16,1024]{3,2,1,0:T(8,128)(2,1)S(1)}) custom-call(s32[1,10]{1,0:T(1,128)S(1)} %copy-done, s32[2]{0:T(128)S(1)} %pad_add_fusion.place, bf16[8,19,16,128]{3,2,1,0:T(8,128)(2,1)S(1)} %all-to-all-done.near, ...), custom_call_target="tpu_custom_call", output_to_operand_aliasing={{0}: (6, {}), {1}: (7, {})} | custom-call | flops 60129542144 | bytes 58720256 | tf_op jit(solution)/shard_map/pallas_call | solution.py:235
  34.2 0.0 collective-permute-done.3.nine
  34.2 0.9 %collective-permute-done.4.ten = bf16[19,16,128]{2,1,0:T(8,128)(2,1)S(1)} collective-permute-done((bf16[19,16,128]{2,1,0:T(8,128)(2,1)S(1)}, bf16[19,16,128]{2,1,0:T(8,128)(2,1)S(1)}, u32[]{:S(2)}, u32[]{:S(2)}) %collective-permute-start.4) | collective-permute-done | bytes 77856 | tf_op jit(solution)/shard_map/ppermute | solution.py:174
  35.1 1.9 %shard_map.52 = (bf16[2,10,16,1024]{3,2,1,0:T(8,128)(2,1)}, bf16[10,16,1024]{2,1,0:T(8,128)(2,1)}) custom-call(s32[1,10]{1,0:T(1,128)S(1)} %copy-done, s32[2]{0:T(128)S(1)} %pad_add_fusion.place, bf16[3,3,16,1024]{3,2,1,0:T(8,128)(2,1)S(1)} %get-tuple-element.17.left, ...), custom_call_target="tpu_custom_call", output_to_operand_aliasing={{0}: (10, {}), {1}: (11, {})} | custom-call | flops 17179869184 | bytes 16777216 | tf_op jit(solution)/shard_map/pallas_call | solution.py:245
  (7 shorter events, 0.0 us)
Async XLA Ops:
  0.6 0.9 %copy-start.1 = (s32[1,16]{1,0:T(1,128)S(1)}, s32[1,16]{1,0:T(1,128)}, u32[]{:S(2)}) copy-start(s32[1,16]{1,0:T(1,128)} %param.4) | copy-start | bytes 196
  3.9 9.8 %collective-permute-start = (bf16[19,16,128]{2,1,0:T(8,128)(2,1)S(1)}, bf16[19,16,128]{2,1,0:T(8,128)(2,1)S(1)}, u32[]{:S(2)}, u32[]{:S(2)}) collective-permute-start(bf16[19,16,128]{2,1,0:T(8,128)(2,1)S(1)} %pad_maximum_fusion.own), channel_id=1, source_target_pairs={{16,0},{18,2},{20,4},{22,6},{24,8},{26,10},{28,12},{30,14},{32,16}... | collective-permute-start | bytes 233480 | tf_op jit(solution)/shard_map/ppermute | solution.py:174
  7.6 20.5 %collective-permute-start.1 = (bf16[19,16,128]{2,1,0:T(8,128)(2,1)S(1)}, bf16[19,16,128]{2,1,0:T(8,128)(2,1)S(1)}, u32[]{:S(2)}, u32[]{:S(2)}) collective-permute-start(bf16[19,16,128]{2,1,0:T(8,128)(2,1)S(1)} %pad_maximum_fusion.own), channel_id=1, source_target_pairs={{80,62},{144,126},{208,190},{272,254},{336,318},{400,382},{464,446... | collective-permute-start | bytes 233480 | tf_op jit(solution)/shard_map/ppermute | solution.py:174
  8.3 19.8 %collective-permute-start.2 = (bf16[19,16,128]{2,1,0:T(8,128)(2,1)S(1)}, bf16[19,16,128]{2,1,0:T(8,128)(2,1)S(1)}, u32[]{:S(2)}, u32[]{:S(2)}) collective-permute-start(bf16[19,16,128]{2,1,0:T(8,128)(2,1)S(1)} %pad_maximum_fusion.own), channel_id=1, source_target_pairs={{80,60},{82,62},{144,124},{146,126},{208,188},{210,190},{272,252},... | collective-permute-start | bytes 233480 | tf_op jit(solution)/shard_map/ppermute | solution.py:174
  14.6 13.5 %copy-start = (s32[1,10]{1,0:T(1,128)S(1)}, s32[1,10]{1,0:T(1,128)}, u32[]{:S(2)}) copy-start(s32[1,10]{1,0:T(1,128)} %order.5) | copy-start | bytes 124
  14.6 17.2 %all-to-all-start = ((bf16[8,19,16,128]{3,2,1,0:T(8,128)(2,1)}), bf16[8,19,16,128]{3,2,1,0:T(8,128)(2,1)S(1)}, u32[]{:S(2)}, u32[]{:S(2)}) async-start(bf16[8,19,16,128]{3,2,1,0:T(8,128)(2,1)} %broadcast_select_fusion), calls=%async_computation | async-start | bytes 1245184 | tf_op jit(solution)/shard_map/all_to_all | solution.py:199
  21.9 12.3 %collective-permute-start.3 = (bf16[19,16,128]{2,1,0:T(8,128)(2,1)S(1)}, bf16[19,16,128]{2,1,0:T(8,128)(2,1)S(1)}, u32[]{:S(2)}, u32[]{:S(2)}) collective-permute-start(bf16[19,16,128]{2,1,0:T(8,128)(2,1)S(1)} %collective-permute-done.eight), channel_id=1, source_target_pairs={{2,0},{4,2},{6,4},{8,6},{10,8},{12,10},{14,12},{16,14},{18,16},{20... | collective-permute-start | bytes 233480 | tf_op jit(solution)/shard_map/ppermute | solution.py:174
  24.1 11.0 %collective-permute-start.4 = (bf16[19,16,128]{2,1,0:T(8,128)(2,1)S(1)}, bf16[19,16,128]{2,1,0:T(8,128)(2,1)S(1)}, u32[]{:S(2)}, u32[]{:S(2)}) collective-permute-start(bf16[19,16,128]{2,1,0:T(8,128)(2,1)S(1)} %collective-permute-done.eight), channel_id=1, source_target_pairs={{4,0},{6,2},{8,4},{10,6},{12,8},{14,10},{16,12},{18,14},{20,16},{2... | collective-permute-start | bytes 233480 | tf_op jit(solution)/shard_map/ppermute | solution.py:174
